TPU v7x, 32 devices: a whole 2x2x4 slice. The times are simulated.
32 devices in a mesh: groups: 2 (over y), ta: 4 (over z), gz: 2 (over x), gy: 2 (over core).
Axes of the slice: x: 2, y: 2, z: 4, core: 2. Of those that a mesh axis runs over, the one named last changes fastest.
Arguments:
- pseudo: float32 [64, 8, 8, 512], P('groups', 'ta', 'gz', 'gy'), parts along dimension 0, may hold values from -12 to 12
- frame_quat: float32 [32, 8, 8, 512], P('groups', 'ta', 'gz', 'gy'), parts along dimension 0, may hold values from -1 to 1, as said below
- link_phase: float32 [8, 8, 8, 512], P('groups', 'ta', 'gz', 'gy'), parts along dimension 0, may hold values from -3.140625 to 3.140625
- active: int32 [16, 8, 512], P(('groups', 'ta'), 'gz', 'gy'), parts along dimension 0, may hold values 0 or 1
- kernel: float32 [648, 16], replicated, may hold values from -0.25 to 0.25
- bias_hidden: float32 [16], replicated, may hold values from -3 to 3
- readout: float32 [16, 8], replicated, may hold values from -1.5 to 1.5
- bias_out: float32 [8], replicated, may hold values from -3 to 3
Outputs:
- solution: float32 [64, 8, 8, 512], P('groups', 'ta', 'gz', 'gy'), parts along dimension 0
- force_field: float32 [16, 8, 512], P(('groups', 'ta'), 'gz', 'gy'), parts along dimension 0
- grad_kernel: float32 [1296, 16], P('groups'), parts along dimension 0
- grad_hidden: float32 [32], P('groups'), parts along dimension 0
- grad_readout: float32 [32, 8], P('groups'), parts along dimension 0
- grad_out: float32 [16], P('groups'), parts along dimension 0
There are 2 independent parts, one for each index of `groups`. A program takes and returns all parts, laid end to end along the dimension named above; an argument that names none is the same for every part. Nothing has to cross between parts.
Inputs may be any that keep to these rules, and one draw needn't show every extreme that they name: For every site and direction mu the four entries frame_quat[4 mu + j], j = 0..3, have a unit sum of squares.
All inputs are finite; a program needn't handle non-finite values. No bound on the sum of `active` on one device may be relied on, other than what follows from the above.
Results may differ from a plain program's by a relative error of at most 0.0003.
Values sent between devices are 32-bit elements; how exact they have to be, the bound alone decides.
A program may use at most 128 MiB of HBM per device.

v0:
```python
import math

import jax
import jax.numpy as jnp
import numpy as np
from jax import lax
from jax.sharding import PartitionSpec as P

X_LEN = 32
ITERS = 3
KNOTS = 8


PRECISE = lax.Precision.HIGHEST
KAPPAS = (0.12, 0.1)
SLOPE_SHARE = 0.5


def extended(cells, sides, width):
    for axis, dim in sides:
        count = lax.axis_size(axis)
        head = lax.slice_in_dim(cells, 0, width, axis=dim)
        tail = lax.slice_in_dim(cells, cells.shape[dim] - width, cells.shape[dim], axis=dim)
        cells = jnp.concatenate(
            [
                lax.ppermute(tail, axis, [(i, (i + 1) % count) for i in range(count)]),
                cells,
                lax.ppermute(head, axis, [((i + 1) % count, i) for i in range(count)]),
            ],
            axis=dim,
        )
    return cells


def from_behind(block, axis, distance):
    devices = range(lax.axis_size(axis))
    route = [((i - distance) % len(devices), i) for i in devices]
    return lax.ppermute(block, axis, route)


def corner_blocks(upper_right, lower_left):
    matrix = np.zeros((4, 4), dtype=complex)
    matrix[0:2, 2:4] = upper_right
    matrix[2:4, 0:2] = lower_left
    return matrix


def spin_tables():
    identity = np.eye(2, dtype=complex)
    paulis = [
        np.array([[0, 1], [1, 0]], dtype=complex),
        np.array([[0, -1j], [1j, 0]], dtype=complex),
        np.array([[1, 0], [0, -1]], dtype=complex),
    ]
    gammas = [corner_blocks(identity, identity)]
    for pauli_index in (2, 1, 0):
        gammas.append(corner_blocks(-1j * paulis[pauli_index], 1j * paulis[pauli_index]))
    lookup = np.zeros((2, 4, 2, 4, 4))
    for direction in range(4):
        for side_index in range(2):
            projector = np.eye(4) + (2 * side_index - 1) * gammas[direction]
            lookup[side_index, direction, 0] = projector.real
            lookup[side_index, direction, 1] = projector.imag
    return lookup


def spin_apply(side_index, direction, vector):
    table = spin_tables()
    real_part = jnp.asarray(table[side_index, direction, 0], jnp.float32)
    imag_part = jnp.asarray(table[side_index, direction, 1], jnp.float32)
    vec_re = vector[:, :, :, 0]
    vec_im = vector[:, :, :, 1]
    out_re = jnp.einsum("ab,fb...->fa...", real_part, vec_re, precision=PRECISE) - jnp.einsum(
        "ab,fb...->fa...", imag_part, vec_im, precision=PRECISE
    )
    out_im = jnp.einsum("ab,fb...->fa...", real_part, vec_im, precision=PRECISE) + jnp.einsum(
        "ab,fb...->fa...", imag_part, vec_re, precision=PRECISE
    )
    return jnp.stack([out_re, out_im], axis=3)


def colour_apply(quadruple, vector, adjoint):
    alpha_re, alpha_im, beta_re, beta_im = (quadruple[0], quadruple[1], quadruple[2], quadruple[3])
    up_re, up_im = (vector[:, :, 0, 0], vector[:, :, 0, 1])
    low_re, low_im = (vector[:, :, 1, 0], vector[:, :, 1, 1])
    if adjoint:
        top_re = alpha_re * up_re + alpha_im * up_im - beta_re * low_re + beta_im * low_im
        top_im = alpha_re * up_im - alpha_im * up_re - beta_re * low_im - beta_im * low_re
        bottom_re = beta_re * up_re + beta_im * up_im + alpha_re * low_re - alpha_im * low_im
        bottom_im = beta_re * up_im - beta_im * up_re + alpha_re * low_im + alpha_im * low_re
    else:
        top_re = alpha_re * up_re - alpha_im * up_im + beta_re * low_re - beta_im * low_im
        top_im = alpha_re * up_im + alpha_im * up_re + beta_re * low_im + beta_im * low_re
        bottom_re = -(beta_re * up_re + beta_im * up_im) + alpha_re * low_re + alpha_im * low_im
        bottom_im = -(beta_re * up_im - beta_im * up_re) + alpha_re * low_im - alpha_im * low_re
    upper_row = jnp.stack([top_re, top_im], axis=2)
    lower_row = jnp.stack([bottom_re, bottom_im], axis=2)
    return jnp.stack([upper_row, lower_row], axis=2)


def along_rows(tensor, stride):
    positions = jnp.arange(tensor.shape[-1]) % X_LEN
    if stride > 0:
        return jnp.where(
            positions == X_LEN - 1,
            jnp.roll(tensor, X_LEN - 1, axis=-1),
            jnp.roll(tensor, -1, axis=-1),
        )
    return jnp.where(
        positions == 0, jnp.roll(tensor, 1 - X_LEN, axis=-1), jnp.roll(tensor, 1, axis=-1)
    )


def region_view(tensor, shift_t, shift_z, shift_y):
    span_t = tensor.shape[-3] - 2
    span_z = tensor.shape[-2] - 2
    span_yx = tensor.shape[-1] - 2 * X_LEN
    start_y = (1 + shift_y) * X_LEN
    return tensor[
        ...,
        1 + shift_t : 1 + shift_t + span_t,
        1 + shift_z : 1 + shift_z + span_z,
        start_y : start_y + span_yx,
    ]


def wilson(spinor, gauge_ext, adjoint):
    vector = spinor.reshape((2, 4, 2, 2) + spinor.shape[1:])
    quaternions = gauge_ext.reshape((4, 4) + gauge_ext.shape[1:])
    centre = region_view(vector, 0, 0, 0)
    gauge_here = region_view(quaternions, 0, 0, 0)
    forward_side = 1 if adjoint else 0
    hopping = jnp.zeros_like(centre)
    for direction in range(4):
        if direction < 3:
            unit_step = [0, 0, 0]
            unit_step[direction] = 1
            ahead_vec = region_view(vector, unit_step[0], unit_step[1], unit_step[2])
            behind = region_view(vector, -unit_step[0], -unit_step[1], -unit_step[2])
            gauge_behind = region_view(
                quaternions[direction], -unit_step[0], -unit_step[1], -unit_step[2]
            )
        else:
            ahead_vec = along_rows(centre, 1)
            behind = along_rows(centre, -1)
            gauge_behind = along_rows(gauge_here[direction], -1)
        forward = colour_apply(gauge_here[direction], ahead_vec, False)
        backward = colour_apply(gauge_behind, behind, True)
        hopping = (
            hopping
            + spin_apply(forward_side, direction, forward)
            + spin_apply(1 - forward_side, direction, backward)
        )
    kappas = jnp.asarray(KAPPAS, jnp.float32).reshape((2, 1, 1, 1, 1, 1, 1))
    result = centre - kappas * hopping
    return result.reshape((32,) + result.shape[4:])


def rotate_one(quadruple, theta_field):
    cosine = jnp.cos(theta_field)
    sine_part = jnp.sin(theta_field)
    return jnp.stack(
        [
            cosine * quadruple[0] - sine_part * quadruple[1],
            cosine * quadruple[1] + sine_part * quadruple[0],
            cosine * quadruple[2] - sine_part * quadruple[3],
            cosine * quadruple[3] + sine_part * quadruple[2],
        ],
        axis=0,
    )


def rotate_links(frame_quat, angles):
    return jnp.concatenate(
        [
            rotate_one(frame_quat[4 * direction : 4 * direction + 4], angles[direction])
            for direction in range(4)
        ],
        axis=0,
    )


def bspline(offsets):
    distance = jnp.abs(offsets)
    outer_part = jnp.maximum(2.0 - distance, 0.0)
    inner_part = jnp.maximum(1.0 - distance, 0.0)
    return (outer_part**3 - 4.0 * inner_part**3) / 6.0


def bspline_slope(offsets):
    distance = jnp.abs(offsets)
    outer_part = jnp.maximum(2.0 - distance, 0.0)
    inner_part = jnp.maximum(1.0 - distance, 0.0)
    return jnp.sign(offsets) * (4.0 * inner_part**2 - outer_part**2) / 2.0


def spline_basis(time_angle):
    position = KNOTS * (time_angle + math.pi) / (2.0 * math.pi)
    knot_index = jnp.arange(KNOTS, dtype=jnp.float32).reshape((KNOTS,) + (1,) * time_angle.ndim)
    offsets = jnp.mod(position[None] - knot_index + KNOTS / 2.0, KNOTS) - KNOTS / 2.0
    return (bspline(offsets), bspline_slope(offsets))


def conditioner_inputs(link_phase, active):
    frozen = 1.0 - active.astype(jnp.float32)
    channels = []
    for direction in range(4):
        if direction == 0:
            channels.append(jnp.cos(link_phase[direction]) * frozen)
            channels.append(jnp.sin(link_phase[direction]) * frozen)
        else:
            channels.append(jnp.cos(link_phase[direction]))
            channels.append(jnp.sin(link_phase[direction]))
    return jnp.stack(channels, axis=0)


def tap_rows(padded, block_index):
    shift_t = block_index // 9 - 1
    shift_z = block_index // 3 % 3 - 1
    shift_y = block_index % 3 - 1
    centre = region_view(padded, shift_t, shift_z, shift_y)
    return jnp.concatenate([along_rows(centre, -1), centre, along_rows(centre, 1)], axis=0)


def conv_forward(padded, kernel, bias_hidden):
    summed = None
    for block_index in range(27):
        rows_in = tap_rows(padded, block_index)
        part_sum = jnp.einsum(
            "ci,c...->i...",
            kernel[24 * block_index : 24 * block_index + 24],
            rows_in,
            precision=PRECISE,
        )
        summed = part_sum if summed is None else summed + part_sum
    return summed + bias_hidden[:, None, None, None]


def coupling_forward(padded, time_angle, active_float, kernel, bias_hidden, readout, bias_out):
    hidden = jnp.tanh(conv_forward(padded, kernel, bias_hidden))
    squashed = jnp.tanh(
        jnp.einsum("ik,i...->k...", readout, hidden, precision=PRECISE)
        + bias_out[:, None, None, None]
    )
    coeffs = SLOPE_SHARE * 2.0 * math.pi / KNOTS * squashed
    values, slopes = spline_basis(time_angle)
    moved_angle = time_angle + active_float * jnp.sum(coeffs * values, axis=0)
    jacobian = 1.0 + active_float * (KNOTS / (2.0 * math.pi)) * jnp.sum(coeffs * slopes, axis=0)
    return (hidden, squashed, values, slopes, moved_angle, jacobian)


def coupling_backward(
    padded,
    hidden,
    squashed,
    values,
    slopes,
    jacobian,
    active_float,
    force_field,
    readout,
    root_volume,
):
    ratio_const = KNOTS / (2.0 * math.pi)
    scale_const = SLOPE_SHARE * 2.0 * math.pi / KNOTS
    coeff_grad = (
        active_float * (force_field * values - ratio_const * slopes / jacobian) / root_volume
    )
    logit_grad = coeff_grad * scale_const * (1.0 - squashed * squashed)
    readout_part = jnp.einsum("i...,k...->ik", hidden, logit_grad, precision=PRECISE)
    out_part = jnp.sum(logit_grad, axis=(1, 2, 3))
    pre_grad = jnp.einsum("ik,k...->i...", readout, logit_grad, precision=PRECISE) * (
        1.0 - hidden * hidden
    )
    hidden_part = jnp.sum(pre_grad, axis=(1, 2, 3))
    kernel_part = jnp.concatenate(
        [
            jnp.einsum("c...,i...->ci", tap_rows(padded, block_index), pre_grad, precision=PRECISE)
            for block_index in range(27)
        ],
        axis=0,
    )
    return (kernel_part, hidden_part, readout_part, out_part)


def time_pairing(time_angle, frame_quat, solution, solution_ahead, eta_field, eta_ahead):
    quadruple = rotate_one(frame_quat[0:4], time_angle)
    split_shape = (2, 4, 2, 2) + solution.shape[1:]
    forward = spin_apply(0, 0, colour_apply(quadruple, solution_ahead.reshape(split_shape), False))
    backward = spin_apply(1, 0, colour_apply(quadruple, solution.reshape(split_shape), True))
    kappas = jnp.asarray(KAPPAS, jnp.float32).reshape((2, 1, 1, 1, 1, 1, 1))
    return -jnp.sum(
        kappas
        * (eta_field.reshape(split_shape) * forward + eta_ahead.reshape(split_shape) * backward)
    )


def flavour_dot(first_field, second_field):
    return jnp.sum((first_field * second_field).reshape((2, -1)), axis=1)


def per_component(scalars):
    return jnp.repeat(scalars, 16).reshape((32, 1, 1, 1))


def extend(tensor, margin, antiperiodic):
    face_ext = extended(tensor, (("ta", 1), ("gz", 2)), margin)
    padded = extended(face_ext, (("gy", 3),), margin * X_LEN)
    if antiperiodic:
        t_count = lax.axis_size("ta")
        at_start = lax.axis_index("ta") == 0
        at_end = lax.axis_index("ta") == t_count - 1
        time_rows = jnp.arange(padded.shape[1])
        flipped = (time_rows < margin) & at_start | (time_rows >= padded.shape[1] - margin) & at_end
        parity = jnp.where(flipped, -1.0, 1.0).astype(jnp.float32).reshape((1, -1, 1, 1))
        padded = padded * parity
    return padded


def normal_apply(spinor, gauge_near):
    applied = wilson(extend(spinor, 1, True), gauge_near, False)
    return wilson(extend(applied, 1, True), gauge_near, True)


def global_norm(residual):
    return lax.psum(flavour_dot(residual, residual), ("ta", "gz", "gy"))


def on_device(pseudo, frame_quat, link_phase, active, kernel, bias_hidden, readout, bias_out):
    active_float = active.astype(jnp.float32)
    padded_inputs = extend(conditioner_inputs(link_phase, active), 1, False)
    hidden, squashed, values, slopes, moved_angle, jacobian = coupling_forward(
        padded_inputs, link_phase[0], active_float, kernel, bias_hidden, readout, bias_out
    )
    angles = jnp.concatenate([moved_angle[None], link_phase[1:]], axis=0)
    gauge_core = rotate_links(frame_quat, angles)
    gauge_near = extend(gauge_core, 1, False)
    solution = jnp.zeros_like(pseudo)
    residual = pseudo
    direction_field = pseudo
    norm_now = global_norm(residual)
    for iteration in range(ITERS):
        applied = normal_apply(direction_field, gauge_near)
        product = lax.psum(flavour_dot(direction_field, applied), ("ta", "gz", "gy"))
        step_len = norm_now / product
        solution = solution + per_component(step_len) * direction_field
        residual = residual - per_component(step_len) * applied
        if iteration + 1 < ITERS:
            norm_next = global_norm(residual)
            direction_field = residual + per_component(norm_next / norm_now) * direction_field
            norm_now = norm_next
    eta_field = wilson(extend(solution, 1, True), gauge_near, False)
    front_plane = jnp.concatenate([solution[:, 0:1], eta_field[:, 0:1]], axis=0)
    incoming = from_behind(front_plane, "ta", -1)
    at_end = lax.axis_index("ta") == lax.axis_size("ta") - 1
    incoming = incoming * jnp.where(at_end, -1.0, 1.0).astype(jnp.float32)
    solution_ahead = jnp.concatenate([solution[:, 1:], incoming[0:32]], axis=1)
    eta_ahead = jnp.concatenate([eta_field[:, 1:], incoming[32:64]], axis=1)

    def pairing(time_angle):
        return time_pairing(time_angle, frame_quat, solution, solution_ahead, eta_field, eta_ahead)

    force_field = -2.0 * jax.grad(pairing)(moved_angle)
    volume = active.size * lax.axis_size("ta") * lax.axis_size("gz") * lax.axis_size("gy")
    root_volume = math.sqrt(volume)
    kernel_part, hidden_part, readout_part, out_part = coupling_backward(
        padded_inputs,
        hidden,
        squashed,
        values,
        slopes,
        jacobian,
        active_float,
        force_field,
        readout,
        root_volume,
    )
    grad_kernel, grad_hidden, grad_readout, grad_out = lax.psum(
        (kernel_part, hidden_part, readout_part, out_part), ("ta", "gz", "gy")
    )
    return (solution, force_field, grad_kernel, grad_hidden, grad_readout, grad_out)


def solution(mesh):
    return jax.shard_map(
        on_device,
        mesh=mesh,
        in_specs=(
            P("groups", "ta", "gz", "gy"),
            P("groups", "ta", "gz", "gy"),
            P("groups", "ta", "gz", "gy"),
            P(("groups", "ta"), "gz", "gy"),
            P(),
            P(),
            P(),
            P(),
        ),
        out_specs=(
            P("groups", "ta", "gz", "gy"),
            P(("groups", "ta"), "gz", "gy"),
            P("groups", None),
            P("groups"),
            P("groups", None),
            P("groups"),
        ),
        check_vma=False,
    )
```

profile of v0, /device:TPU:0, one launch (start us, length us, event | category | flops | bytes accessed | tf_op | source)
XLA Modules:
  0.0 561.8 jit_solution(13198876812897579343)
XLA Ops:
  6.9 3.1 collective-permute-start.6
  10.0 2.1 collective-permute-start.7
  13.1 3.8 collective-permute-start.1
  17.1 1.7 collective-permute-start.8
  21.0 1.6 collective-permute-done.9
  46.0 1.5 fusion.453
  48.8 4.2 collective-permute-start.13
  53.1 2.4 collective-permute-done.12
  56.0 1.7 collective-permute-start.15
  58.3 1.7 collective-permute-start.3
  60.6 1.4 collective-permute-done.15
  62.9 1.6 collective-permute-done.2
  64.5 1.4 collective-permute-done.3
  88.4 4.0 collective-permute-start.19
  92.4 4.1 collective-permute-done.18
  99.4 3.7 collective-permute-done.20
  103.0 1.4 collective-permute-done.21
  127.0 31.9 %all-reduce.13 = (f32[2]{0:T(128)S(1)}, f32[2]{0:T(128)S(1)}) all-reduce(f32[2]{0:T(128)S(1)} %reduce_sum.443, f32[2]{0:T(128)S(1)} %reduce_sum.450), channel_id=1, replica_groups=mesh['groups'=2,'ta'=4,'gz'=2,'gy'=2] {'ta','gz','gy'}, use_global_device_ids=true, to_apply=%region_2.3 | all-reduce | flops 4 | bytes 32 | tf_op jit(solution)/shard_map/psum | solution.py:326
  159.8 29.6 %psum.72 = f32[2]{0:T(128)S(1)} all-reduce(f32[2]{0:T(128)S(1)} %reduce_sum.456), channel_id=1, replica_groups=mesh['groups'=2,'ta'=4,'gz'=2,'gy'=2] {'ta','gz','gy'}, use_global_device_ids=true, to_apply=%region_9.10 | all-reduce | flops 2 | bytes 16 | tf_op jit(solution)/shard_map/psum | solution.py:326
  190.3 4.0 collective-permute-start.25
  194.2 4.2 collective-permute-done.24
  198.8 2.0 collective-permute-start.27
  200.8 2.9 collective-permute-done.26
  203.7 1.4 collective-permute-done.27
  227.2 3.8 collective-permute-start.31
  231.0 4.3 collective-permute-done.30
  235.3 1.6 collective-permute-done.31
  237.5 1.7 collective-permute-start.33
  239.2 4.4 collective-permute-done.32
  243.6 1.4 collective-permute-done.33
  267.2 29.9 %psum.73 = f32[2]{0:T(128)S(1)} all-reduce(f32[2]{0:T(128)S(1)} %reduce_sum.462), channel_id=1, replica_groups=mesh['groups'=2,'ta'=4,'gz'=2,'gy'=2] {'ta','gz','gy'}, use_global_device_ids=true, to_apply=%region_12.13 | all-reduce | flops 2 | bytes 16 | tf_op jit(solution)/shard_map/psum | solution.py:344
  298.6 29.5 %psum.74 = f32[2]{0:T(128)S(1)} all-reduce(f32[2]{0:T(128)S(1)} %reduce_sum.468), channel_id=1, replica_groups=mesh['groups'=2,'ta'=4,'gz'=2,'gy'=2] {'ta','gz','gy'}, use_global_device_ids=true, to_apply=%region_15.16 | all-reduce | flops 2 | bytes 16 | tf_op jit(solution)/shard_map/psum | solution.py:326
  330.9 4.2 collective-permute-start.37
  335.1 4.0 collective-permute-done.36
  339.7 2.0 collective-permute-start.39
  341.8 3.0 collective-permute-done.38
  368.1 3.8 collective-permute-start.43
  371.9 4.3 collective-permute-done.42
  378.2 1.7 collective-permute-start.45
  379.9 4.2 collective-permute-done.44
  408.0 30.4 %psum.75 = f32[2]{0:T(128)S(1)} all-reduce(f32[2]{0:T(128)S(1)} %reduce_sum.471), channel_id=1, replica_groups=mesh['groups'=2,'ta'=4,'gz'=2,'gy'=2] {'ta','gz','gy'}, use_global_device_ids=true, to_apply=%region_18.19 | all-reduce | flops 2 | bytes 16 | tf_op jit(solution)/shard_map/psum | solution.py:344
  438.9 4.0 collective-permute-start.49
  442.8 3.6 collective-permute-done.48
  446.7 2.0 collective-permute-start.51
  448.7 2.9 collective-permute-done.50
  475.4 3.2 collective-permute-start.54
  480.3 4.2 collective-permute-done.54
  499.9 61.5 %all-reduce.12 = (f32[648,16]{0,1:T(8,128)}, f32[16]{0:T(128)}, f32[16,8]{0,1:T(8,128)}, f32[8]{0:T(128)}) all-reduce(f32[648,16]{0,1:T(8,128)S(1)} %concatenate.1110, f32[16]{0:T(128)S(1)} %get-tuple-element.807, f32[16,8]{0,1:T(8,128)S(1)} %convolution_bitcast_fusion.38, ...), channel_id=1, replica_groups=mesh['groups'=2,'ta'=4,'gz'=2,'gy'=2] {'ta','gz','gy'}, use_global_device_ids=true, to_apply=%region_52.53 | all-reduce | flops 10520 | bytes 84160 | tf_op jit(solution)/shard_map/psum | solution.py:378
  (1063 shorter events, 221.9 us)
Async XLA Ops:
  6.9 10.1 %collective-permute-start.6 = (f32[8,1,4,256]{3,2,1,0:T(4,128)S(1)}, f32[8,1,4,256]{3,2,1,0:T(4,128)S(1)}, u32[]{:S(2)}, u32[]{:S(2)}) collective-permute-start(f32[8,1,4,256]{3,2,1,0:T(4,128)S(1)} %get-tuple-element.746), channel_id=1, source_target_pairs={{0,4},{4,8},{8,12},{12,0},{1,5},{5,9},{9,13},{13,1},{2,6},{6,10},{... | collective-permute-start | bytes 98312 | tf_op jit(solution)/shard_map/ppermute | solution.py:26
  10.0 7.0 %collective-permute-start.7 = (f32[8,1,4,256]{3,2,1,0:T(4,128)S(1)}, f32[8,1,4,256]{3,2,1,0:T(4,128)S(1)}, u32[]{:S(2)}, u32[]{:S(2)}) collective-permute-start(f32[8,1,4,256]{3,2,1,0:T(4,128)S(1)} %get-tuple-element.747), channel_id=1, source_target_pairs={{4,0},{8,4},{12,8},{0,12},{5,1},{9,5},{13,9},{1,13},{6,2},{10,6},{... | collective-permute-start | bytes 98312 | tf_op jit(solution)/shard_map/ppermute | solution.py:28
  13.0 39.9 %collective-permute-start = (f32[32,1,4,256]{3,2,1,0:T(4,128)S(1)}, f32[32,1,4,256]{3,2,1,0:T(4,128)S(1)}, u32[]{:S(2)}, u32[]{:S(2)}) collective-permute-start(f32[32,1,4,256]{3,2,1,0:T(4,128)S(1)} %get-tuple-element.621), channel_id=1, source_target_pairs={{0,4},{4,8},{8,12},{12,0},{1,5},{5,9},{9,13},{13,1},{2,6},{6,10},{... | collective-permute-start | bytes 393224 | tf_op jit(solution)/shard_map/ppermute | solution.py:26
  13.1 39.9 %collective-permute-start.1 = (f32[32,1,4,256]{3,2,1,0:T(4,128)S(1)}, f32[32,1,4,256]{3,2,1,0:T(4,128)S(1)}, u32[]{:S(2)}, u32[]{:S(2)}) collective-permute-start(f32[32,1,4,256]{3,2,1,0:T(4,128)S(1)} %get-tuple-element.620), channel_id=1, source_target_pairs={{4,0},{8,4},{12,8},{0,12},{5,1},{9,5},{13,9},{1,13},{6,2},{10,6},{... | collective-permute-start | bytes 393224 | tf_op jit(solution)/shard_map/ppermute | solution.py:28
  17.1 4.0 collective-permute-start.8
  18.8 3.9 collective-permute-start.9
  48.7 6.8 %collective-permute-start.12 = (f32[16,1,4,256]{3,2,1,0:T(4,128)S(1)}, f32[16,1,4,256]{3,2,1,0:T(4,128)S(1)}, u32[]{:S(2)}, u32[]{:S(2)}) collective-permute-start(f32[16,1,4,256]{3,2,1,0:T(4,128)S(1)} %get-tuple-element.657), channel_id=1, source_target_pairs={{0,4},{4,8},{8,12},{12,0},{1,5},{5,9},{9,13},{13,1},{2,6},{6,10},{... | collective-permute-start | bytes 196616 | tf_op jit(solution)/shard_map/ppermute | solution.py:26
  48.8 6.7 %collective-permute-start.13 = (f32[16,1,4,256]{3,2,1,0:T(4,128)S(1)}, f32[16,1,4,256]{3,2,1,0:T(4,128)S(1)}, u32[]{:S(2)}, u32[]{:S(2)}) collective-permute-start(f32[16,1,4,256]{3,2,1,0:T(4,128)S(1)} %get-tuple-element.658), channel_id=1, source_target_pairs={{4,0},{8,4},{12,8},{0,12},{5,1},{9,5},{13,9},{1,13},{6,2},{10,6},{... | collective-permute-start | bytes 196616 | tf_op jit(solution)/shard_map/ppermute | solution.py:28
  55.6 5.0 collective-permute-start.14
  56.0 6.0 %collective-permute-start.15 = (f32[16,4,1,256]{3,2,1,0:T(1,128)S(1)}, f32[16,4,1,256]{3,2,1,0:T(1,128)S(1)}, u32[]{:S(2)}, u32[]{:S(2)}) collective-permute-start(f32[16,4,1,256]{3,2,1,0:T(1,128)S(1)} %get-tuple-element.539), channel_id=1, source_target_pairs={{2,0},{0,2},{3,1},{1,3},{6,4},{4,6},{7,5},{5,7},{10,8},{8,10},{11,... | collective-permute-start | bytes 196616 | tf_op jit(solution)/shard_map/ppermute | solution.py:28
  57.9 6.6 %collective-permute-start.2 = (f32[32,4,1,256]{3,2,1,0:T(1,128)S(1)}, f32[32,4,1,256]{3,2,1,0:T(1,128)S(1)}, u32[]{:S(2)}, u32[]{:S(2)}) collective-permute-start(f32[32,4,1,256]{3,2,1,0:T(1,128)S(1)} %get-tuple-element.366), channel_id=1, source_target_pairs={{0,2},{2,0},{1,3},{3,1},{4,6},{6,4},{5,7},{7,5},{8,10},{10,8},{9,1... | collective-permute-start | bytes 393224 | tf_op jit(solution)/shard_map/ppermute | solution.py:26
  58.3 7.6 %collective-permute-start.3 = (f32[32,4,1,256]{3,2,1,0:T(1,128)S(1)}, f32[32,4,1,256]{3,2,1,0:T(1,128)S(1)}, u32[]{:S(2)}, u32[]{:S(2)}) collective-permute-start(f32[32,4,1,256]{3,2,1,0:T(1,128)S(1)} %get-tuple-element.367), channel_id=1, source_target_pairs={{2,0},{0,2},{3,1},{1,3},{6,4},{4,6},{7,5},{5,7},{10,8},{8,10},{11,... | collective-permute-start | bytes 393224 | tf_op jit(solution)/shard_map/ppermute | solution.py:28
  62.3 5.3 collective-permute-start.16
  62.4 5.2 collective-permute-start.17
  66.5 2.6 collective-permute-start.4
  66.6 2.8 collective-permute-start.5
  88.3 8.2 %collective-permute-start.18 = (f32[32,1,4,256]{3,2,1,0:T(4,128)S(1)}, f32[32,1,4,256]{3,2,1,0:T(4,128)S(1)}, u32[]{:S(2)}, u32[]{:S(2)}) collective-permute-start(f32[32,1,4,256]{3,2,1,0:T(4,128)S(1)} %get-tuple-element.534), channel_id=1, source_target_pairs={{0,4},{4,8},{8,12},{12,0},{1,5},{5,9},{9,13},{13,1},{2,6},{6,10},{... | collective-permute-start | bytes 393224 | tf_op jit(solution)/shard_map/ppermute | solution.py:26
  88.4 8.7 %collective-permute-start.19 = (f32[32,1,4,256]{3,2,1,0:T(4,128)S(1)}, f32[32,1,4,256]{3,2,1,0:T(4,128)S(1)}, u32[]{:S(2)}, u32[]{:S(2)}) collective-permute-start(f32[32,1,4,256]{3,2,1,0:T(4,128)S(1)} %get-tuple-element.535), channel_id=1, source_target_pairs={{4,0},{8,4},{12,8},{0,12},{5,1},{9,5},{13,9},{1,13},{6,2},{10,6},{... | collective-permute-start | bytes 393224 | tf_op jit(solution)/shard_map/ppermute | solution.py:28
  97.3 5.8 %collective-permute-start.20 = (f32[32,4,1,256]{3,2,1,0:T(1,128)S(1)}, f32[32,4,1,256]{3,2,1,0:T(1,128)S(1)}, u32[]{:S(2)}, u32[]{:S(2)}) collective-permute-start(f32[32,4,1,256]{3,2,1,0:T(1,128)S(1)} %get-tuple-element.362), channel_id=1, source_target_pairs={{0,2},{2,0},{1,3},{3,1},{4,6},{6,4},{5,7},{7,5},{8,10},{10,8},{9,1... | collective-permute-start | bytes 393224 | tf_op jit(solution)/shard_map/ppermute | solution.py:26
  98.3 6.1 %collective-permute-start.21 = (f32[32,4,1,256]{3,2,1,0:T(1,128)S(1)}, f32[32,4,1,256]{3,2,1,0:T(1,128)S(1)}, u32[]{:S(2)}, u32[]{:S(2)}) collective-permute-start(f32[32,4,1,256]{3,2,1,0:T(1,128)S(1)} %get-tuple-element.363), channel_id=1, source_target_pairs={{2,0},{0,2},{3,1},{1,3},{6,4},{4,6},{7,5},{5,7},{10,8},{8,10},{11,... | collective-permute-start | bytes 393224 | tf_op jit(solution)/shard_map/ppermute | solution.py:28
  105.1 2.6 collective-permute-start.23
  190.2 8.3 %collective-permute-start.24 = (f32[32,1,4,256]{3,2,1,0:T(4,128)S(1)}, f32[32,1,4,256]{3,2,1,0:T(4,128)S(1)}, u32[]{:S(2)}, u32[]{:S(2)}) collective-permute-start(f32[32,1,4,256]{3,2,1,0:T(4,128)S(1)} %get-tuple-element.532), channel_id=1, source_target_pairs={{0,4},{4,8},{8,12},{12,0},{1,5},{5,9},{9,13},{13,1},{2,6},{6,10},{... | collective-permute-start | bytes 393224 | tf_op jit(solution)/shard_map/ppermute | solution.py:26
  190.3 8.2 %collective-permute-start.25 = (f32[32,1,4,256]{3,2,1,0:T(4,128)S(1)}, f32[32,1,4,256]{3,2,1,0:T(4,128)S(1)}, u32[]{:S(2)}, u32[]{:S(2)}) collective-permute-start(f32[32,1,4,256]{3,2,1,0:T(4,128)S(1)} %get-tuple-element.533), channel_id=1, source_target_pairs={{4,0},{8,4},{12,8},{0,12},{5,1},{9,5},{13,9},{1,13},{6,2},{10,6},{... | collective-permute-start | bytes 393224 | tf_op jit(solution)/shard_map/ppermute | solution.py:28
  198.7 5.0 collective-permute-start.26
  198.8 6.4 %collective-permute-start.27 = (f32[32,4,1,256]{3,2,1,0:T(1,128)S(1)}, f32[32,4,1,256]{3,2,1,0:T(1,128)S(1)}, u32[]{:S(2)}, u32[]{:S(2)}) collective-permute-start(f32[32,4,1,256]{3,2,1,0:T(1,128)S(1)} %get-tuple-element.361), channel_id=1, source_target_pairs={{2,0},{0,2},{3,1},{1,3},{6,4},{4,6},{7,5},{5,7},{10,8},{8,10},{11,... | collective-permute-start | bytes 393224 | tf_op jit(solution)/shard_map/ppermute | solution.py:28
  205.8 2.6 collective-permute-start.29
  227.1 8.2 %collective-permute-start.30 = (f32[32,1,4,256]{3,2,1,0:T(4,128)S(1)}, f32[32,1,4,256]{3,2,1,0:T(4,128)S(1)}, u32[]{:S(2)}, u32[]{:S(2)}) collective-permute-start(f32[32,1,4,256]{3,2,1,0:T(4,128)S(1)} %get-tuple-element.530), channel_id=1, source_target_pairs={{0,4},{4,8},{8,12},{12,0},{1,5},{5,9},{9,13},{13,1},{2,6},{6,10},{... | collective-permute-start | bytes 393224 | tf_op jit(solution)/shard_map/ppermute | solution.py:26
  227.2 9.7 %collective-permute-start.31 = (f32[32,1,4,256]{3,2,1,0:T(4,128)S(1)}, f32[32,1,4,256]{3,2,1,0:T(4,128)S(1)}, u32[]{:S(2)}, u32[]{:S(2)}) collective-permute-start(f32[32,1,4,256]{3,2,1,0:T(4,128)S(1)} %get-tuple-element.531), channel_id=1, source_target_pairs={{4,0},{8,4},{12,8},{0,12},{5,1},{9,5},{13,9},{1,13},{6,2},{10,6},{... | collective-permute-start | bytes 393224 | tf_op jit(solution)/shard_map/ppermute | solution.py:28
  237.1 6.5 %collective-permute-start.32 = (f32[32,4,1,256]{3,2,1,0:T(1,128)S(1)}, f32[32,4,1,256]{3,2,1,0:T(1,128)S(1)}, u32[]{:S(2)}, u32[]{:S(2)}) collective-permute-start(f32[32,4,1,256]{3,2,1,0:T(1,128)S(1)} %get-tuple-element.358), channel_id=1, source_target_pairs={{0,2},{2,0},{1,3},{3,1},{4,6},{6,4},{5,7},{7,5},{8,10},{10,8},{9,1... | collective-permute-start | bytes 393224 | tf_op jit(solution)/shard_map/ppermute | solution.py:26
  237.5 7.5 %collective-permute-start.33 = (f32[32,4,1,256]{3,2,1,0:T(1,128)S(1)}, f32[32,4,1,256]{3,2,1,0:T(1,128)S(1)}, u32[]{:S(2)}, u32[]{:S(2)}) collective-permute-start(f32[32,4,1,256]{3,2,1,0:T(1,128)S(1)} %get-tuple-element.359), channel_id=1, source_target_pairs={{2,0},{0,2},{3,1},{1,3},{6,4},{4,6},{7,5},{5,7},{10,8},{8,10},{11,... | collective-permute-start | bytes 393224 | tf_op jit(solution)/shard_map/ppermute | solution.py:28
  245.6 2.0 collective-permute-start.34
  245.7 2.6 collective-permute-start.35
  330.9 8.2 %collective-permute-start.36 = (f32[32,1,4,256]{3,2,1,0:T(4,128)S(1)}, f32[32,1,4,256]{3,2,1,0:T(4,128)S(1)}, u32[]{:S(2)}, u32[]{:S(2)}) collective-permute-start(f32[32,1,4,256]{3,2,1,0:T(4,128)S(1)} %get-tuple-element.528), channel_id=1, source_target_pairs={{0,4},{4,8},{8,12},{12,0},{1,5},{5,9},{9,13},{13,1},{2,6},{6,10},{... | collective-permute-start | bytes 393224 | tf_op jit(solution)/shard_map/ppermute | solution.py:26
  330.9 8.5 %collective-permute-start.37 = (f32[32,1,4,256]{3,2,1,0:T(4,128)S(1)}, f32[32,1,4,256]{3,2,1,0:T(4,128)S(1)}, u32[]{:S(2)}, u32[]{:S(2)}) collective-permute-start(f32[32,1,4,256]{3,2,1,0:T(4,128)S(1)} %get-tuple-element.529), channel_id=1, source_target_pairs={{4,0},{8,4},{12,8},{0,12},{5,1},{9,5},{13,9},{1,13},{6,2},{10,6},{... | collective-permute-start | bytes 393224 | tf_op jit(solution)/shard_map/ppermute | solution.py:28
  339.7 5.1 collective-permute-start.38
  339.7 6.4 %collective-permute-start.39 = (f32[32,4,1,256]{3,2,1,0:T(1,128)S(1)}, f32[32,4,1,256]{3,2,1,0:T(1,128)S(1)}, u32[]{:S(2)}, u32[]{:S(2)}) collective-permute-start(f32[32,4,1,256]{3,2,1,0:T(1,128)S(1)} %get-tuple-element.357), channel_id=1, source_target_pairs={{2,0},{0,2},{3,1},{1,3},{6,4},{4,6},{7,5},{5,7},{10,8},{8,10},{11,... | collective-permute-start | bytes 393224 | tf_op jit(solution)/shard_map/ppermute | solution.py:28
  346.8 2.6 collective-permute-start.41
  368.0 8.2 %collective-permute-start.42 = (f32[32,1,4,256]{3,2,1,0:T(4,128)S(1)}, f32[32,1,4,256]{3,2,1,0:T(4,128)S(1)}, u32[]{:S(2)}, u32[]{:S(2)}) collective-permute-start(f32[32,1,4,256]{3,2,1,0:T(4,128)S(1)} %get-tuple-element.526), channel_id=1, source_target_pairs={{0,4},{4,8},{8,12},{12,0},{1,5},{5,9},{9,13},{13,1},{2,6},{6,10},{... | collective-permute-start | bytes 393224 | tf_op jit(solution)/shard_map/ppermute | solution.py:26
  368.1 9.5 %collective-permute-start.43 = (f32[32,1,4,256]{3,2,1,0:T(4,128)S(1)}, f32[32,1,4,256]{3,2,1,0:T(4,128)S(1)}, u32[]{:S(2)}, u32[]{:S(2)}) collective-permute-start(f32[32,1,4,256]{3,2,1,0:T(4,128)S(1)} %get-tuple-element.527), channel_id=1, source_target_pairs={{4,0},{8,4},{12,8},{0,12},{5,1},{9,5},{13,9},{1,13},{6,2},{10,6},{... | collective-permute-start | bytes 393224 | tf_op jit(solution)/shard_map/ppermute | solution.py:28
  377.8 6.3 %collective-permute-start.44 = (f32[32,4,1,256]{3,2,1,0:T(1,128)S(1)}, f32[32,4,1,256]{3,2,1,0:T(1,128)S(1)}, u32[]{:S(2)}, u32[]{:S(2)}) collective-permute-start(f32[32,4,1,256]{3,2,1,0:T(1,128)S(1)} %get-tuple-element.354), channel_id=1, source_target_pairs={{0,2},{2,0},{1,3},{3,1},{4,6},{6,4},{5,7},{7,5},{8,10},{10,8},{9,1... | collective-permute-start | bytes 393224 | tf_op jit(solution)/shard_map/ppermute | solution.py:26
  378.2 7.3 %collective-permute-start.45 = (f32[32,4,1,256]{3,2,1,0:T(1,128)S(1)}, f32[32,4,1,256]{3,2,1,0:T(1,128)S(1)}, u32[]{:S(2)}, u32[]{:S(2)}) collective-permute-start(f32[32,4,1,256]{3,2,1,0:T(1,128)S(1)} %get-tuple-element.355), channel_id=1, source_target_pairs={{2,0},{0,2},{3,1},{1,3},{6,4},{4,6},{7,5},{5,7},{10,8},{8,10},{11,... | collective-permute-start | bytes 393224 | tf_op jit(solution)/shard_map/ppermute | solution.py:28
  386.2 2.6 collective-permute-start.47
  438.8 7.6 %collective-permute-start.48 = (f32[32,1,4,256]{3,2,1,0:T(4,128)S(1)}, f32[32,1,4,256]{3,2,1,0:T(4,128)S(1)}, u32[]{:S(2)}, u32[]{:S(2)}) collective-permute-start(f32[32,1,4,256]{3,2,1,0:T(4,128)S(1)} %get-tuple-element.524), channel_id=1, source_target_pairs={{0,4},{4,8},{8,12},{12,0},{1,5},{5,9},{9,13},{13,1},{2,6},{6,10},{... | collective-permute-start | bytes 393224 | tf_op jit(solution)/shard_map/ppermute | solution.py:26
  438.9 7.5 %collective-permute-start.49 = (f32[32,1,4,256]{3,2,1,0:T(4,128)S(1)}, f32[32,1,4,256]{3,2,1,0:T(4,128)S(1)}, u32[]{:S(2)}, u32[]{:S(2)}) collective-permute-start(f32[32,1,4,256]{3,2,1,0:T(4,128)S(1)} %get-tuple-element.525), channel_id=1, source_target_pairs={{4,0},{8,4},{12,8},{0,12},{5,1},{9,5},{13,9},{1,13},{6,2},{10,6},{... | collective-permute-start | bytes 393224 | tf_op jit(solution)/shard_map/ppermute | solution.py:28
  446.6 5.0 collective-permute-start.50
  446.7 6.4 %collective-permute-start.51 = (f32[32,4,1,256]{3,2,1,0:T(1,128)S(1)}, f32[32,4,1,256]{3,2,1,0:T(1,128)S(1)}, u32[]{:S(2)}, u32[]{:S(2)}) collective-permute-start(f32[32,4,1,256]{3,2,1,0:T(1,128)S(1)} %get-tuple-element.353), channel_id=1, source_target_pairs={{2,0},{0,2},{3,1},{1,3},{6,4},{4,6},{7,5},{5,7},{10,8},{8,10},{11,... | collective-permute-start | bytes 393224 | tf_op jit(solution)/shard_map/ppermute | solution.py:28
  453.7 2.6 collective-permute-start.53
  475.4 9.1 %collective-permute-start.54 = (f32[64,1,4,256]{3,2,1,0:T(4,128)S(1)}, f32[64,1,4,256]{3,2,1,0:T(4,128)S(1)}, u32[]{:S(2)}, u32[]{:S(2)}) collective-permute-start(f32[64,1,4,256]{3,2,1,0:T(4,128)S(1)} %pad_maximum_fusion.12), channel_id=1, source_target_pairs={{4,0},{8,4},{12,8},{0,12},{5,1},{9,5},{13,9},{1,13},{6,2},{10,6},{... | collective-permute-start | bytes 786440 | tf_op jit(solution)/shard_map/ppermute | solution.py:38
  (110 other events, 1200.2 us)
where the time goes:
time: 572 us; the launch traced here: 562 us
  blocking collectives  213 us (37%)
  matrix products  105 us (18%)
  waiting for transfers between devices  81.4 us (14%)
  starting transfers between devices  64.5 us (11%)
  other arithmetic  57.3 us (10%)
  local copies, waits for them, and re-layouts  34.2 us (6%)
  between operations  6.91 us (1%)
    psum x3, blocking collectives, global_norm(): return lax.psum(flavour_dot(residual, residual), ('ta', 'gz', 'gy'))  91 us
    psum x1, blocking collectives, on_device(): lax.psum((kernel_part, hidden_part, readout_part, out_part), ('ta', 'gz',...  61.5 us
    psum x2, blocking collectives, on_device(): lax.psum(flavour_dot(direction_field, applied), ('ta', 'gz', 'gy'))  60.3 us
    ppermute x27, waiting for transfers between devices, extended(): lax.ppermute(tail, axis, [(i, (i + 1) % count) for i in range(count)])  57.2 us
    ppermute x27, starting transfers between devices, extended(): lax.ppermute(head, axis, [((i + 1) % count, i) for i in range(count)])  52.5 us
    dot_general x58, matrix products, spin_apply(): jnp.einsum('ab,fb...->fa...', real_part, vec_re, precision=PRECISE)  22.6 us
    dot_general x58, matrix products, spin_apply(): jnp.einsum('ab,fb...->fa...', real_part, vec_im, precision=PRECISE)  20.9 us
    dot_general x58, matrix products, spin_apply(): jnp.einsum('ab,fb...->fa...', imag_part, vec_im, precision=PRECISE)  20.7 us
  transfers between devices with their start and end apart: 55, of which 44 were waited for; matrix products, arithmetic and copies ran while one was open for 6% of the time, Pallas kernels for 0%

commit v1 on v0

v1 whole, which is shorter than its diff:
```python
import math

import jax
import jax.numpy as jnp
from jax import lax
from jax.experimental import pallas as pl
from jax.experimental.pallas import tpu as pltpu
from jax.sharding import PartitionSpec as P

X_LEN = 32
ITERS = 3
KNOTS = 8


PRECISE = lax.Precision.HIGHEST
KAPPAS = (0.12, 0.1)
SLOPE_SHARE = 0.5


def extended(cells, sides, width):
    for axis, dim in sides:
        count = lax.axis_size(axis)
        head = lax.slice_in_dim(cells, 0, width, axis=dim)
        tail = lax.slice_in_dim(cells, cells.shape[dim] - width, cells.shape[dim], axis=dim)
        cells = jnp.concatenate(
            [
                lax.ppermute(tail, axis, [(i, (i + 1) % count) for i in range(count)]),
                cells,
                lax.ppermute(head, axis, [((i + 1) % count, i) for i in range(count)]),
            ],
            axis=dim,
        )
    return cells


def along_rows(tensor, stride):
    positions = jnp.arange(tensor.shape[-1]) % X_LEN
    if stride > 0:
        return jnp.where(
            positions == X_LEN - 1,
            jnp.roll(tensor, X_LEN - 1, axis=-1),
            jnp.roll(tensor, -1, axis=-1),
        )
    return jnp.where(
        positions == 0, jnp.roll(tensor, 1 - X_LEN, axis=-1), jnp.roll(tensor, 1, axis=-1)
    )


def region_view(tensor, shift_t, shift_z, shift_y):
    span_t = tensor.shape[-3] - 2
    span_z = tensor.shape[-2] - 2
    span_yx = tensor.shape[-1] - 2 * X_LEN
    start_y = (1 + shift_y) * X_LEN
    return tensor[
        ...,
        1 + shift_t : 1 + shift_t + span_t,
        1 + shift_z : 1 + shift_z + span_z,
        start_y : start_y + span_yx,
    ]


def rotate_one(quadruple, theta_field):
    cosine = jnp.cos(theta_field)
    sine_part = jnp.sin(theta_field)
    return jnp.stack(
        [
            cosine * quadruple[0] - sine_part * quadruple[1],
            cosine * quadruple[1] + sine_part * quadruple[0],
            cosine * quadruple[2] - sine_part * quadruple[3],
            cosine * quadruple[3] + sine_part * quadruple[2],
        ],
        axis=0,
    )


def rotate_links(frame_quat, angles):
    return jnp.concatenate(
        [
            rotate_one(frame_quat[4 * direction : 4 * direction + 4], angles[direction])
            for direction in range(4)
        ],
        axis=0,
    )


def bspline(offsets):
    distance = jnp.abs(offsets)
    outer_part = jnp.maximum(2.0 - distance, 0.0)
    inner_part = jnp.maximum(1.0 - distance, 0.0)
    return (outer_part**3 - 4.0 * inner_part**3) / 6.0


def bspline_slope(offsets):
    distance = jnp.abs(offsets)
    outer_part = jnp.maximum(2.0 - distance, 0.0)
    inner_part = jnp.maximum(1.0 - distance, 0.0)
    return jnp.sign(offsets) * (4.0 * inner_part**2 - outer_part**2) / 2.0


def spline_basis(time_angle):
    position = KNOTS * (time_angle + math.pi) / (2.0 * math.pi)
    knot_index = jnp.arange(KNOTS, dtype=jnp.float32).reshape((KNOTS,) + (1,) * time_angle.ndim)
    offsets = jnp.mod(position[None] - knot_index + KNOTS / 2.0, KNOTS) - KNOTS / 2.0
    return (bspline(offsets), bspline_slope(offsets))


def conditioner_inputs(link_phase, active):
    frozen = 1.0 - active.astype(jnp.float32)
    channels = []
    for direction in range(4):
        if direction == 0:
            channels.append(jnp.cos(link_phase[direction]) * frozen)
            channels.append(jnp.sin(link_phase[direction]) * frozen)
        else:
            channels.append(jnp.cos(link_phase[direction]))
            channels.append(jnp.sin(link_phase[direction]))
    return jnp.stack(channels, axis=0)


def tap_rows(padded, block_index):
    shift_t = block_index // 9 - 1
    shift_z = block_index // 3 % 3 - 1
    shift_y = block_index % 3 - 1
    centre = region_view(padded, shift_t, shift_z, shift_y)
    return jnp.concatenate([along_rows(centre, -1), centre, along_rows(centre, 1)], axis=0)


def conv_forward(padded, kernel, bias_hidden):
    summed = None
    for block_index in range(27):
        rows_in = tap_rows(padded, block_index)
        part_sum = jnp.einsum(
            "ci,c...->i...",
            kernel[24 * block_index : 24 * block_index + 24],
            rows_in,
            precision=PRECISE,
        )
        summed = part_sum if summed is None else summed + part_sum
    return summed + bias_hidden[:, None, None, None]


def coupling_forward(padded, time_angle, active_float, kernel, bias_hidden, readout, bias_out):
    hidden = jnp.tanh(conv_forward(padded, kernel, bias_hidden))
    squashed = jnp.tanh(
        jnp.einsum("ik,i...->k...", readout, hidden, precision=PRECISE)
        + bias_out[:, None, None, None]
    )
    coeffs = SLOPE_SHARE * 2.0 * math.pi / KNOTS * squashed
    values, slopes = spline_basis(time_angle)
    moved_angle = time_angle + active_float * jnp.sum(coeffs * values, axis=0)
    jacobian = 1.0 + active_float * (KNOTS / (2.0 * math.pi)) * jnp.sum(coeffs * slopes, axis=0)
    return (hidden, squashed, values, slopes, moved_angle, jacobian)


def coupling_backward(
    padded,
    hidden,
    squashed,
    values,
    slopes,
    jacobian,
    active_float,
    force_field,
    readout,
    root_volume,
):
    ratio_const = KNOTS / (2.0 * math.pi)
    scale_const = SLOPE_SHARE * 2.0 * math.pi / KNOTS
    coeff_grad = (
        active_float * (force_field * values - ratio_const * slopes / jacobian) / root_volume
    )
    logit_grad = coeff_grad * scale_const * (1.0 - squashed * squashed)
    readout_part = jnp.einsum("i...,k...->ik", hidden, logit_grad, precision=PRECISE)
    out_part = jnp.sum(logit_grad, axis=(1, 2, 3))
    pre_grad = jnp.einsum("ik,k...->i...", readout, logit_grad, precision=PRECISE) * (
        1.0 - hidden * hidden
    )
    hidden_part = jnp.sum(pre_grad, axis=(1, 2, 3))
    kernel_part = jnp.concatenate(
        [
            jnp.einsum("c...,i...->ci", tap_rows(padded, block_index), pre_grad, precision=PRECISE)
            for block_index in range(27)
        ],
        axis=0,
    )
    return (kernel_part, hidden_part, readout_part, out_part)


GROUP = ("ta", "gz", "gy")
MESH = pl.DeviceIdType.MESH
F32 = jnp.float32

SPIN_K = {
    1: [[(-1, 0, 1), (1, 0, 0)], [(1, 1, 1), (-1, 1, 0)]],
    2: [[(1, 1, 0), (1, 1, 1)], [(-1, 0, 0), (-1, 0, 1)]],
    3: [[(-1, 1, 1), (1, 1, 0)], [(-1, 0, 1), (1, 0, 0)]],
}
TURN = {0: [[(-1, 0, 0), (-1, 0, 1)], [(-1, 1, 0), (-1, 1, 1)]], **SPIN_K}
BACK = {0: [[(1, 0, 0), (1, 0, 1)], [(1, 1, 0), (1, 1, 1)]], **SPIN_K}


def group_size():
    return lax.axis_size("ta") * lax.axis_size("gz") * lax.axis_size("gy")


def each(count, step):
    if count <= 16:
        for index in range(count):
            step(index)
    else:

        def looped(index, carry):
            step(index)
            return carry

        lax.fori_loop(0, count, looped, 0)


def peer(offset):
    nz, ny = lax.axis_size("gz"), lax.axis_size("gy")
    mine = (lax.axis_index("ta") * nz + lax.axis_index("gz")) * ny + lax.axis_index("gy")
    target = lax.rem(mine + offset, group_size())
    return {
        "groups": lax.axis_index("groups"),
        "ta": target // (nz * ny),
        "gz": lax.rem(target // ny, nz),
        "gy": lax.rem(target, ny),
    }


def greet_group():
    barrier = pltpu.get_barrier_semaphore()
    count = group_size() - 1

    def greet(index):
        pl.semaphore_signal(barrier, inc=1, device_id=peer(index + 1), device_id_type=MESH)

    each(count, greet)
    pl.semaphore_wait(barrier, count)


def step_along(axis, distance):
    count = lax.axis_size(axis)
    return {axis: lax.rem(lax.axis_index(axis) + (distance + count), count)}


def rows_of(shape):
    return lax.broadcasted_iota(jnp.int32, shape, len(shape) - 2)


def lanes_of(shape):
    return lax.broadcasted_iota(jnp.int32, shape, len(shape) - 1)


def turned(tensor, shift, axis):
    size = tensor.shape[axis]
    shift = shift % size
    return tensor if shift == 0 else pltpu.roll(tensor, shift, axis)


def colour_forward(quad, half):
    a_re, a_im, b_re, b_im = quad
    result = []
    for spin in range(2):
        (u_re, u_im), (l_re, l_im) = half[spin]
        result.append(
            [
                [
                    a_re * u_re - a_im * u_im + b_re * l_re - b_im * l_im,
                    a_re * u_im + a_im * u_re + b_re * l_im + b_im * l_re,
                ],
                [
                    a_re * l_re + a_im * l_im - b_re * u_re - b_im * u_im,
                    a_re * l_im - a_im * l_re - b_re * u_im + b_im * u_re,
                ],
            ]
        )
    return result


def colour_adjoint(quad, half):
    a_re, a_im, b_re, b_im = quad
    result = []
    for spin in range(2):
        (u_re, u_im), (l_re, l_im) = half[spin]
        result.append(
            [
                [
                    a_re * u_re + a_im * u_im - b_re * l_re + b_im * l_im,
                    a_re * u_im - a_im * u_re - b_re * l_im - b_im * l_re,
                ],
                [
                    b_re * u_re + b_im * u_im + a_re * l_re - a_im * l_im,
                    b_re * u_im - b_im * u_re + a_re * l_im + a_im * l_re,
                ],
            ]
        )
    return result


def project(field, mu, sign):
    half = []
    for spin in range(2):
        colours = []
        for colour in range(2):
            parts = []
            for part in range(2):
                flip, s, r = TURN[mu][spin][part]
                upper, lower = field[spin, colour, part], field[2 + s, colour, r]
                parts.append(upper + lower if flip * sign > 0 else upper - lower)
            colours.append(parts)
        half.append(colours)
    return half


def along_x(tensor, stride):
    place = lax.rem(lanes_of(tensor.shape), X_LEN)
    if stride > 0:
        return jnp.where(place == X_LEN - 1, turned(tensor, X_LEN - 1, 2), turned(tensor, -1, 2))
    return jnp.where(place == 0, turned(tensor, 1 - X_LEN, 2), turned(tensor, 1, 2))


def each_part():
    return [(s, c, r) for s in range(2) for c in range(2) for r in range(2)]


def cg_kernel(
    pseudo_ref,
    gauge_ref,
    sol_ref,
    force_ref,
    links,
    bank,
    dvec,
    xs,
    es,
    out,
    hop,
    t_send,
    t_recv,
    z_send,
    z_recv,
    y_send,
    y_recv,
    f_send,
    f_recv,
    ratio,
    red_send,
    red_recv,
    halo_ssem,
    halo_rsem,
    f_ssem,
    f_rsem,
    red_ssem,
    red_rsem,
):
    nt, nz, width = pseudo_ref.shape[-3:]
    shape = (2, nt * nz, width)
    others = group_size() - 1
    row, lane = rows_of(shape), lanes_of(shape)
    z_place = lax.rem(row, nz)
    t_low = row < (nt - 1) * nz
    y_count = width // X_LEN
    kappa = jnp.where(lax.broadcasted_iota(jnp.int32, shape, 0) == 0, KAPPAS[0], KAPPAS[1]).astype(F32)
    last_sign = jnp.where(lax.axis_index("ta") == lax.axis_size("ta") - 1, -1.0, 1.0).astype(F32)
    first_sign = jnp.where(lax.axis_index("ta") == 0, -1.0, 1.0).astype(F32)

    for mu in range(4):
        for part in range(4):
            for t in range(nt):
                links[mu, part, t * nz : (t + 1) * nz] = gauge_ref[mu, part, t]
    for flavour in range(2):
        for s in range(4):
            for c in range(2):
                for r in range(2):
                    for t in range(nt):
                        rows = slice(t * nz, (t + 1) * nz)
                        bank[0, s, c, r, flavour, rows] = pseudo_ref[flavour, s, c, r, t]
    for s in range(4):
        zero = jnp.zeros((2, 2) + shape, F32)
        bank[1, s] = zero
        dvec[s] = zero
        xs[s] = zero
        es[s] = zero
        out[s] = zero
    ratio[...] = jnp.ones(ratio.shape, F32)

    greet_group()

    def reduce_copy(parity, index):
        return pltpu.make_async_remote_copy(
            src_ref=red_send.at[parity],
            dst_ref=red_recv.at[parity, index],
            send_sem=red_ssem.at[parity, index],
            recv_sem=red_rsem.at[parity, index],
            device_id=peer(index + 1),
            device_id_type=MESH,
        )

    def start_sum(parity, total):
        folded = total[:, :, 0:128]
        for start in range(128, width, 128):
            folded = folded + total[:, :, start : start + 128]
        sums = jnp.sum(folded, axis=1, keepdims=True)
        tile_row = rows_of((8, 128))
        red_send[parity] = jnp.where(tile_row == 0, sums[0], jnp.where(tile_row == 1, sums[1], 0.0))
        each(others, lambda index: reduce_copy(parity, index).start())

    def finish_sum(parity):
        each(others, lambda index: reduce_copy(parity, index).wait())
        total = red_send[parity] + jnp.sum(red_recv[parity], axis=0)
        total = jnp.broadcast_to(jnp.sum(total, axis=1, keepdims=True), (8, 128))
        return jnp.where(rows_of((8, 128)) < 2, total, 1.0)

    def spread(pair):
        return jnp.stack([jnp.broadcast_to(pair[f : f + 1, 0:1], shape[1:]) for f in range(2)])

    def halo_copy(side, parity):
        send, recv, axis = ((t_send, t_recv, "ta"), (z_send, z_recv, "gz"), (y_send, y_recv, "gy"))[side // 2]
        return pltpu.make_async_remote_copy(
            src_ref=send.at[side % 2],
            dst_ref=recv.at[parity, side % 2],
            send_sem=halo_ssem.at[side],
            recv_sem=halo_rsem.at[parity, side],
            device_id=step_along(axis, -1 if side % 2 == 0 else 1),
            device_id_type=MESH,
        )

    def pack_t(half, ahead, send):
        for s, c in ((0, 0), (0, 1), (1, 0), (1, 1)):
            first, second = half[s][c]
            moved = [turned(v, -nz if ahead else nz, 1) for v in (first, second)]
            if ahead:
                send[2 * s + c] = jnp.where(row < nz, second, moved[0]) if nt == 2 else None
            else:
                send[2 * s + c] = jnp.where(row < nz, moved[0], second)
            yield s, c, moved

    def place_t(halo, moved, ahead, part):
        if ahead:
            edge = halo if part == 0 else turned(halo, nz, 1)
            return jnp.where(t_low, moved, edge)
        edge = halo if part == 0 else turned(halo, nz, 1)
        return jnp.where(row < nz, edge, moved)

    def send_halos(field, parity):
        for mu in range(3):
            for back in range(2):
                half = project(field, mu, -1 if back else 1)
                if back:
                    half = colour_adjoint([links[mu, p] for p in range(4)], half)
                side = 2 * mu + back
                if mu == 0:
                    for s, c, moved in pack_t(half, not back, t_send.at[back]):
                        for r in range(2):
                            hop[side, s, c, r] = moved[r]
                elif mu == 1:
                    packed = [None, None]
                    for s, c, r in each_part():
                        value = half[s][c][r]
                        hop[side, s, c, r] = turned(value, 1 if back else -1, 1)
                        slot = 2 * s + c
                        put = turned(value, slot - (nz - 1) if back else slot, 1)
                        packed[r] = put if packed[r] is None else jnp.where(z_place == slot, put, packed[r])
                    for r in range(2):
                        z_send[back, r] = packed[r]
                else:
                    packed = None
                    for s, c, r in each_part():
                        value = half[s][c][r]
                        hop[side, s, c, r] = turned(value, X_LEN if back else -X_LEN, 2)
                        slot = 4 * s + 2 * c + r
                        put = turned(value, (slot - (y_count - 1) if back else slot) * X_LEN, 2)
                        packed = put if packed is None else jnp.where(lane // X_LEN == slot, put, packed)
                    y_send[back] = packed
                halo_copy(side, parity).start()

    def add_hop(total, half, mu, back):
        sign = 1 if back else -1
        for s, c, r in each_part():
            flip, source, part = BACK[mu][s][r]
            top, low = half[s][c][r], half[source][c][part]
            if total[s][c][r] is None:
                total[s][c][r] = top
                total[2 + s][c][r] = low if flip * sign > 0 else -low
            else:
                total[s][c][r] = total[s][c][r] + top
                lower = total[2 + s][c][r]
                total[2 + s][c][r] = lower + low if flip * sign > 0 else lower - low

    def turned_wilson(source, parity):
        field = {
            (s, c, r): bank[source, s, c, r] for s in range(4) for c in range(2) for r in range(2)
        }
        send_halos(field, parity)
        total = [[[None, None], [None, None]] for _ in range(4)]
        quad = [links[3, p] for p in range(4)]
        half = project(field, 3, 1)
        ahead = [[[along_x(half[s][c][r], 1) for r in range(2)] for c in range(2)] for s in range(2)]
        add_hop(total, colour_forward(quad, ahead), 3, False)
        half = colour_adjoint(quad, project(field, 3, -1))
        behind = [[[along_x(half[s][c][r], -1) for r in range(2)] for c in range(2)] for s in range(2)]
        add_hop(total, behind, 3, True)
        for s in range(4):
            for c in range(2):
                for r in range(2):
                    out[s, c, r] = total[s][c][r]
        for mu in (2, 1, 0):
            total = [[[out[s, c, r] for r in range(2)] for c in range(2)] for s in range(4)]
            for back in range(2):
                side = 2 * mu + back
                halo_copy(side, parity).wait()
                half = [[[None, None], [None, None]] for _ in range(2)]
                for s, c, r in each_part():
                    moved = hop[side, s, c, r]
                    if mu == 0:
                        halo = t_recv[parity, back, 2 * s + c] * (first_sign if back else last_sign)
                        merged = place_t(halo, moved, not back, r)
                    elif mu == 1:
                        slot = 2 * s + c
                        halo = z_recv[parity, back, r]
                        if back:
                            merged = jnp.where(z_place == 0, turned(halo, -slot, 1), moved)
                        else:
                            merged = jnp.where(z_place == nz - 1, turned(halo, nz - 1 - slot, 1), moved)
                    else:
                        slot = 4 * s + 2 * c + r
                        halo = y_recv[parity, back]
                        if back:
                            merged = jnp.where(lane < X_LEN, turned(halo, -slot * X_LEN, 2), moved)
                        else:
                            placed = turned(halo, (y_count - 1 - slot) * X_LEN, 2)
                            merged = jnp.where(lane >= width - X_LEN, placed, moved)
                    half[s][c][r] = merged
                if not back:
                    half = colour_forward([links[mu, p] for p in range(4)], half)
                add_hop(total, half, mu, back)
            for s in range(4):
                for c in range(2):
                    for r in range(2):
                        value = total[s][c][r]
                        if mu == 0:
                            value = bank[source, s, c, r] - kappa * value
                            value = value if s < 2 else -value
                        out[s, c, r] = value

    def iteration(k, carry):
        start_sum(0, sum(jnp.sum(bank[0, s] * bank[0, s], axis=(0, 1)) for s in range(4)))
        turned_wilson(0, 0)
        norm = finish_sum(0)
        growth = spread(jnp.where(k > 0, norm / ratio[...], 0.0))
        ratio[...] = norm
        square = jnp.zeros(shape, F32)
        for s in range(4):
            image = out[s] + growth * bank[1, s]
            bank[1, s] = image
            dvec[s] = bank[0, s] + growth * dvec[s]
            square = square + jnp.sum(image * image, axis=(0, 1))
        start_sum(1, square)

        @pl.when(k < ITERS - 1)
        def _():
            turned_wilson(1, 1)

        length = spread(ratio[...] / finish_sum(1))
        for s in range(4):
            xs[s] = xs[s] + length * dvec[s]
            es[s] = es[s] + length * bank[1, s]
            bank[0, s] = bank[0, s] - length * out[s]
        return carry

    lax.fori_loop(0, ITERS, iteration, 0)

    def front_copy(which):
        return pltpu.make_async_remote_copy(
            src_ref=f_send.at[which],
            dst_ref=f_recv.at[which],
            send_sem=f_ssem.at[which],
            recv_sem=f_rsem.at[which],
            device_id=step_along("ta", -1),
            device_id_type=MESH,
        )

    for which, held in enumerate((xs, es)):
        half = project({(s, c, r): held[s, c, r] for s in range(4) for c in range(2) for r in range(2)}, 0, 1)
        for s, c, moved in pack_t(half, True, f_send.at[which]):
            for r in range(2):
                hop[which, s, c, r] = moved[r]
        front_copy(which).start()
    for flavour in range(2):
        for s in range(4):
            for c in range(2):
                for r in range(2):
                    for t in range(nt):
                        sol_ref[flavour, s, c, r, t] = xs[s, c, r, flavour, t * nz : (t + 1) * nz]
    force = jnp.zeros(shape, F32)
    for which, held in enumerate((es, xs)):
        front_copy(which).wait()
        half = [[[None, None], [None, None]] for _ in range(2)]
        for s, c, r in each_part():
            half[s][c][r] = place_t(f_recv[which, 2 * s + c] * last_sign, hop[which, s, c, r], True, r)
        image = colour_forward([links[0, p] for p in range(4)], half)
        for s in range(2):
            for c in range(2):
                left = [held[s, c, r] + held[2 + s, c, r] for r in range(2)]
                term = left[1] * image[s][c][0] - left[0] * image[s][c][1]
                force = force + term if c == 0 else force - term
    force = force * (2.0 * kappa)
    force = force[0] + force[1]
    for t in range(nt):
        force_ref[t] = force[t * nz : (t + 1) * nz]


def conjugate_gradient(pseudo, gauge):
    nt, nz, width = pseudo.shape[1:]
    rows = nt * nz
    others = group_size() - 1
    field = (4, 2, 2, 2, rows, width)
    vmem = lambda *dims: pltpu.VMEM(dims, F32)
    dma = lambda *dims: pltpu.SemaphoreType.DMA(dims)
    sol, force = pl.pallas_call(
        cg_kernel,
        out_shape=(
            jax.ShapeDtypeStruct((2, 4, 2, 2, nt, nz, width), F32),
            jax.ShapeDtypeStruct((nt, nz, width), F32),
        ),
        in_specs=[pl.BlockSpec(memory_space=pltpu.VMEM)] * 2,
        out_specs=[pl.BlockSpec(memory_space=pltpu.VMEM)] * 2,
        scratch_shapes=[
            vmem(4, 4, rows, width),
            vmem(2, *field),
            vmem(*field),
            vmem(*field),
            vmem(*field),
            vmem(*field),
            vmem(6, 2, 2, 2, 2, rows, width),
            vmem(2, 4, 2, rows, width),
            vmem(2, 2, 4, 2, rows, width),
            vmem(2, 2, 2, rows, width),
            vmem(2, 2, 2, 2, rows, width),
            vmem(2, 2, rows, width),
            vmem(2, 2, 2, rows, width),
            vmem(2, 4, 2, rows, width),
            vmem(2, 4, 2, rows, width),
            vmem(8, 128),
            vmem(2, 8, 128),
            vmem(2, others, 8, 128),
            dma(6),
            dma(2, 6),
            dma(2),
            dma(2),
            dma(2, others),
            dma(2, others),
        ],
        compiler_params=pltpu.CompilerParams(
            collective_id=0, has_side_effects=True, vmem_limit_bytes=32 * 1024 * 1024
        ),
    )(pseudo.reshape((2, 4, 2, 2, nt, nz, width)), gauge.reshape((4, 4, nt, nz, width)))
    return sol.reshape(pseudo.shape), force


def sum_kernel(data_ref, out_ref, landed, reduced, ssem, rsem, gather_ssem, gather_rsem):
    count = group_size()
    chunk = data_ref.shape[0] // count
    nz, ny = lax.axis_size("gz"), lax.axis_size("gy")
    mine = (lax.axis_index("ta") * nz + lax.axis_index("gz")) * ny + lax.axis_index("gy")
    greet_group()

    def part_of(device):
        return pl.ds(pl.multiple_of(device * chunk, 8), chunk)

    def scatter(index):
        return pltpu.make_async_remote_copy(
            src_ref=data_ref.at[part_of(lax.rem(mine + index + 1, count))],
            dst_ref=landed.at[index],
            send_sem=ssem.at[index],
            recv_sem=rsem.at[index],
            device_id=peer(index + 1),
            device_id_type=MESH,
        )

    def gather(index, owner):
        return pltpu.make_async_remote_copy(
            src_ref=reduced,
            dst_ref=out_ref.at[part_of(owner)],
            send_sem=gather_ssem.at[index],
            recv_sem=gather_rsem.at[index],
            device_id=peer(index + 1),
            device_id_type=MESH,
        )

    each(count - 1, lambda index: scatter(index).start())
    each(count - 1, lambda index: scatter(index).wait())
    total = data_ref[part_of(mine)] + jnp.sum(landed[...], axis=0)
    reduced[...] = total
    each(count - 1, lambda index: gather(index, mine).start())
    out_ref[part_of(mine)] = total
    each(count - 1, lambda index: gather(index, lax.rem(mine + count - index - 1, count)).wait())


def group_sum(arrays):
    count = group_size()
    flat = jnp.concatenate([a.reshape(-1) for a in arrays])
    chunk = -(-flat.size // (count * 1024)) * 8
    data = jnp.pad(flat, (0, count * chunk * 128 - flat.size)).reshape((count * chunk, 128))
    dma = lambda *dims: pltpu.SemaphoreType.DMA(dims)
    summed = pl.pallas_call(
        sum_kernel,
        out_shape=jax.ShapeDtypeStruct(data.shape, F32),
        in_specs=[pl.BlockSpec(memory_space=pltpu.VMEM)],
        out_specs=pl.BlockSpec(memory_space=pltpu.VMEM),
        scratch_shapes=[
            pltpu.VMEM((count - 1, chunk, 128), F32),
            pltpu.VMEM((chunk, 128), F32),
            dma(count - 1),
            dma(count - 1),
            dma(count - 1),
            dma(count - 1),
        ],
        compiler_params=pltpu.CompilerParams(
            collective_id=1, has_side_effects=True, vmem_limit_bytes=32 * 1024 * 1024
        ),
    )(data).reshape(-1)
    results, start = [], 0
    for a in arrays:
        results.append(summed[start : start + a.size].reshape(a.shape))
        start += a.size
    return results


def extend(tensor, margin):
    face_ext = extended(tensor, (("ta", 1), ("gz", 2)), margin)
    return extended(face_ext, (("gy", 3),), margin * X_LEN)


def on_device(pseudo, frame_quat, link_phase, active, kernel, bias_hidden, readout, bias_out):
    active_float = active.astype(jnp.float32)
    padded_inputs = extend(conditioner_inputs(link_phase, active), 1)
    hidden, squashed, values, slopes, moved_angle, jacobian = coupling_forward(
        padded_inputs, link_phase[0], active_float, kernel, bias_hidden, readout, bias_out
    )
    angles = jnp.concatenate([moved_angle[None], link_phase[1:]], axis=0)
    gauge_core = rotate_links(frame_quat, angles)
    solution, force_field = conjugate_gradient(pseudo, gauge_core)
    root_volume = math.sqrt(active.size * group_size())
    kernel_part, hidden_part, readout_part, out_part = coupling_backward(
        padded_inputs,
        hidden,
        squashed,
        values,
        slopes,
        jacobian,
        active_float,
        force_field,
        readout,
        root_volume,
    )
    grad_kernel, grad_hidden, grad_readout, grad_out = group_sum(
        (kernel_part, hidden_part, readout_part, out_part)
    )
    return (solution, force_field, grad_kernel, grad_hidden, grad_readout, grad_out)


def solution(mesh):
    return jax.shard_map(
        on_device,
        mesh=mesh,
        in_specs=(
            P("groups", "ta", "gz", "gy"),
            P("groups", "ta", "gz", "gy"),
            P("groups", "ta", "gz", "gy"),
            P(("groups", "ta"), "gz", "gy"),
            P(),
            P(),
            P(),
            P(),
        ),
        out_specs=(
            P("groups", "ta", "gz", "gy"),
            P(("groups", "ta"), "gz", "gy"),
            P("groups", None),
            P("groups"),
            P("groups", None),
            P("groups"),
        ),
        check_vma=False,
    )
```

time: 572 us -> 114 us (0.20); the launches traced: 562 us -> 114 us
  blocking collectives: 213 us -> 0 us
  matrix products: 105 us -> 19 us
  waiting for transfers between devices: 81.4 us -> 5.5 us
  starting transfers between devices: 64.5 us -> 7.83 us
  Pallas kernels: 0 us -> 56.4 us
  other arithmetic: 57.3 us -> 10.1 us
  local copies, waits for them, and re-layouts: 34.2 us -> 13.4 us
    psum x6 -> x0, blocking collectives: 213 us -> none  [the longest x3 91 us: global_norm(): return lax.psum(flavour_dot(residual, residual), ('ta', 'gz', 'gy'))]
    dot_general x232 -> x0, matrix products: 84.9 us -> none  [the longest x58 22.6 us: spin_apply(): jnp.einsum('ab,fb...->fa...', real_part, vec_re, precision=PRECISE)]
    pallas_call x0 -> x2, Pallas kernels: none -> 56.4 us  [the longest x1 44.2 us: conjugate_gradient(): pl.pallas_call(cg_kernel, out_shape=(jax.ShapeDtypeStruct((2, 4, 2, 2, nt...]
    ppermute x27 -> x3, waiting for transfers between devices: 57.2 us -> 3.58 us  [extended(): lax.ppermute(tail, axis, [(i, (i + 1) % count) for i in range(count)])]
    ppermute x27 -> x3, starting transfers between devices: 52.5 us -> 3.12 us  [extended(): lax.ppermute(head, axis, [((i + 1) % count, i) for i in range(count)])]
    ppermute x27 -> x3, waiting for transfers between devices: 19.9 us -> 1.92 us  [extended(): lax.ppermute(head, axis, [((i + 1) % count, i) for i in range(count)])]
    sub x60 -> x0, other arithmetic: 14.5 us -> none  [the longest x26 6.13 us: colour_apply(): alpha_re * up_im - alpha_im * up_re - beta_re * low_im - beta_im * low_re]
    mul x14 -> x0, other arithmetic: 7.96 us -> none  [the longest x7 6.32 us: extend(): padded = padded * parity]
  transfers between devices with their start and end apart: 55 -> 6, of which waited for: 44 -> 6; matrix products, arithmetic and copies ran while one was open for 6% -> 1% of each run, Pallas kernels for 0% -> 0%
where the time goes in v1:
time: 114 us
  Pallas kernels  56.4 us (49%)
  matrix products  19 us (17%)
  local copies, waits for them, and re-layouts  13.4 us (12%)
  other arithmetic  10.1 us (9%)
  starting transfers between devices  7.83 us (7%)
  waiting for transfers between devices  5.5 us (5%)
  between operations  1.49 us (1%)
    pallas_call x1, Pallas kernels, conjugate_gradient(): pl.pallas_call(cg_kernel, out_shape=(jax.ShapeDtypeStruct((2, 4, 2, 2, nt...  44.2 us
    pallas_call x1, Pallas kernels, group_sum(): pl.pallas_call(sum_kernel, out_shape=jax.ShapeDtypeStruct(data.shape, F32...  12.2 us
    dot_general x27, matrix products, coupling_backward(): jnp.einsum('c...,i...->ci', tap_rows(padded, block_index), pre_grad, prec...  9.58 us
    dot_general x27, matrix products, conv_forward(): jnp.einsum('ci,c...->i...', kernel[24 * block_index:24 * block_index + 24...  8.47 us
    unnamed x30, local copies, waits for them, and re-layouts  6.17 us
    ppermute x3, starting transfers between devices, extended(): lax.ppermute(tail, axis, [(i, (i + 1) % count) for i in range(count)])  4.7 us
    ppermute x3, waiting for transfers between devices, extended(): lax.ppermute(tail, axis, [(i, (i + 1) % count) for i in range(count)])  3.58 us
    ppermute x3, starting transfers between devices, extended(): lax.ppermute(head, axis, [((i + 1) % count, i) for i in range(count)])  3.12 us
  transfers between devices with their start and end apart: 6, of which 6 were waited for; matrix products, arithmetic and copies ran while one was open for 1% of the time, Pallas kernels for 0%

profile of v1, /device:TPU:0, one launch (start us, length us, event | category | flops | bytes accessed | tf_op | source)
XLA Modules:
  0.0 113.7 jit_solution(7445488622960210484)
XLA Ops:
  0.7 0.8 constant_dynamic-update-slice_fusion.7
  1.5 0.8 constant_dynamic-update-slice_fusion.6
  2.8 3.1 %collective-permute-start = (f32[8,1,4,256]{3,2,1,0:T(4,128)S(1)}, f32[8,1,4,256]{3,2,1,0:T(4,128)S(1)}, u32[]{:S(2)}, u32[]{:S(2)}) collective-permute-start(f32[8,1,4,256]{3,2,1,0:T(4,128)S(1)} %get-tuple-element.294), channel_id=1, source_target_pairs={{0,4},{4,8},{8,12},{12,0},{1,5},{5,9},{9,13},{13,1},{2,6},{6,10},{... | collective-permute-start | bytes 98312 | tf_op jit(solution)/shard_map/ppermute | solution.py:27
  5.9 2.1 %collective-permute-start.1 = (f32[8,1,4,256]{3,2,1,0:T(4,128)S(1)}, f32[8,1,4,256]{3,2,1,0:T(4,128)S(1)}, u32[]{:S(2)}, u32[]{:S(2)}) collective-permute-start(f32[8,1,4,256]{3,2,1,0:T(4,128)S(1)} %get-tuple-element.295), channel_id=1, source_target_pairs={{4,0},{8,4},{12,8},{0,12},{5,1},{9,5},{13,9},{1,13},{6,2},{10,6},{... | collective-permute-start | bytes 98312 | tf_op jit(solution)/shard_map/ppermute | solution.py:29
  8.0 1.9 %collective-permute-done = f32[8,1,4,256]{3,2,1,0:T(4,128)S(1)} collective-permute-done((f32[8,1,4,256]{3,2,1,0:T(4,128)S(1)}, f32[8,1,4,256]{3,2,1,0:T(4,128)S(1)}, u32[]{:S(2)}, u32[]{:S(2)}) %collective-permute-start) | collective-permute-done | bytes 32800 | tf_op jit(solution)/shard_map/ppermute | solution.py:27
  10.2 1.6 %collective-permute-start.2 = (f32[8,4,1,256]{3,2,1,0:T(1,128)S(1)}, f32[8,4,1,256]{3,2,1,0:T(1,128)S(1)}, u32[]{:S(2)}, u32[]{:S(2)}) collective-permute-start(f32[8,4,1,256]{3,2,1,0:T(1,128)S(1)} %get-tuple-element.245), channel_id=1, source_target_pairs={{0,2},{2,0},{1,3},{3,1},{4,6},{6,4},{5,7},{7,5},{8,10},{10,8},{9,1... | collective-permute-start | bytes 98312 | tf_op jit(solution)/shard_map/ppermute | solution.py:27
  11.8 0.5 collective-permute-start.3
  13.1 1.1 collective-permute-done.2
  14.2 1.5 %collective-permute-done.3 = f32[8,4,1,256]{3,2,1,0:T(1,128)S(1)} collective-permute-done((f32[8,4,1,256]{3,2,1,0:T(1,128)S(1)}, f32[8,4,1,256]{3,2,1,0:T(1,128)S(1)}, u32[]{:S(2)}, u32[]{:S(2)}) %collective-permute-start.3) | collective-permute-done | bytes 32800 | tf_op jit(solution)/shard_map/ppermute | solution.py:29
  17.4 0.5 collective-permute-start.5
  18.1 0.6 collective-permute-done.4
  18.9 0.4 pad_maximum_fusion
  19.3 0.7 fusion.175
  20.0 0.7 fusion.176
  20.7 0.4 fusion.179
  21.1 0.4 fusion.178
  21.5 0.4 fusion.177
  24.0 0.7 copy-done.3
  30.4 0.5 maximum_select_fusion.45
  37.8 0.6 copy-done.6
  38.7 0.6 copy-done.7
  39.6 0.6 copy-done.4
  41.5 44.2 %shard_map.127 = (f32[2,4,2,2,2,4,256]{6,5,4,3,2,1,0:T(4,128)S(1)}, f32[2,4,256]{2,1,0:T(4,128)S(1)}) custom-call(f32[2,4,2,2,2,4,256]{6,5,4,3,2,1,0:T(4,128)S(1)} %bitcast.429, f32[4,4,2,4,256]{4,3,2,1,0:T(4,128)S(1)} %bitcast.431), custom_call_target="tpu_custom_call" | custom-call | tf_op jit(solution)/shard_map/pallas_call | solution.py:621
  86.2 0.5 fusion.197
  87.0 0.4 convolution_bitcast_fusion.13
  87.3 0.4 convolution_bitcast_fusion.14
  87.7 0.4 convolution_bitcast_fusion.15
  88.0 0.4 convolution_bitcast_fusion.16
  88.4 0.4 convolution_bitcast_fusion.17
  89.5 0.4 convolution_bitcast_fusion.20
  89.8 0.4 convolution_bitcast_fusion.21
  90.2 0.4 convolution_bitcast_fusion.22
  90.5 0.4 convolution_bitcast_fusion.23
  90.9 0.4 convolution_bitcast_fusion.24
  91.3 0.4 convolution_bitcast_fusion.25
  91.6 0.4 convolution_bitcast_fusion.26
  92.7 0.4 convolution_bitcast_fusion.29
  93.0 0.4 convolution_bitcast_fusion.30
  93.4 0.4 convolution_bitcast_fusion.31
  93.8 0.4 convolution_bitcast_fusion.32
  96.9 12.2 %shard_map.128 = f32[128,128]{1,0:T(8,128)S(1)} custom-call(f32[128,128]{1,0:T(8,128)S(1)} %pad_bitcast_fusion.data_ref), custom_call_target="tpu_custom_call" | custom-call | tf_op jit(solution)/shard_map/pallas_call | solution.py:707
  109.1 0.6 slice.1850
  109.7 0.5 slice.2121
  110.2 0.6 slice.2123
  110.8 0.7 copy.124
  111.7 0.8 copy.123
  112.4 0.7 copy.323
  113.1 0.6 copy.324
  (160 shorter events, 24.8 us)
Async XLA Ops:
  0.6 38.1 %copy-start = (f32[16,8]{0,1:T(8,128)S(1)}, f32[16,8]{0,1:T(8,128)}, u32[]{:S(2)}) copy-start(f32[16,8]{0,1:T(8,128)} %param.14) | copy-start | bytes 1540
  0.6 1.6 %copy-start.2 = (f32[4,2,4,256]{3,2,1,0:T(4,128)S(1)}, f32[4,2,4,256]{3,2,1,0:T(4,128)}, u32[]{:S(2)}) copy-start(f32[4,2,4,256]{3,2,1,0:T(4,128)} %param.10) | copy-start | bytes 98308
  2.8 5.2 %copy-start.5 = (s32[2,4,256]{2,1,0:T(4,128)S(1)}, s32[2,4,256]{2,1,0:T(4,128)}, u32[]{:S(2)}) copy-start(s32[2,4,256]{2,1,0:T(4,128)} %param.11) | copy-start | bytes 24580
  2.8 7.1 %collective-permute-start = (f32[8,1,4,256]{3,2,1,0:T(4,128)S(1)}, f32[8,1,4,256]{3,2,1,0:T(4,128)S(1)}, u32[]{:S(2)}, u32[]{:S(2)}) collective-permute-start(f32[8,1,4,256]{3,2,1,0:T(4,128)S(1)} %get-tuple-element.294), channel_id=1, source_target_pairs={{0,4},{4,8},{8,12},{12,0},{1,5},{5,9},{9,13},{13,1},{2,6},{6,10},{... | collective-permute-start | bytes 98312 | tf_op jit(solution)/shard_map/ppermute | solution.py:27
  5.9 4.3 %collective-permute-start.1 = (f32[8,1,4,256]{3,2,1,0:T(4,128)S(1)}, f32[8,1,4,256]{3,2,1,0:T(4,128)S(1)}, u32[]{:S(2)}, u32[]{:S(2)}) collective-permute-start(f32[8,1,4,256]{3,2,1,0:T(4,128)S(1)} %get-tuple-element.295), channel_id=1, source_target_pairs={{4,0},{8,4},{12,8},{0,12},{5,1},{9,5},{13,9},{1,13},{6,2},{10,6},{... | collective-permute-start | bytes 98312 | tf_op jit(solution)/shard_map/ppermute | solution.py:29
  10.2 4.0 %collective-permute-start.2 = (f32[8,4,1,256]{3,2,1,0:T(1,128)S(1)}, f32[8,4,1,256]{3,2,1,0:T(1,128)S(1)}, u32[]{:S(2)}, u32[]{:S(2)}) collective-permute-start(f32[8,4,1,256]{3,2,1,0:T(1,128)S(1)} %get-tuple-element.245), channel_id=1, source_target_pairs={{0,2},{2,0},{1,3},{3,1},{4,6},{6,4},{5,7},{7,5},{8,10},{10,8},{9,1... | collective-permute-start | bytes 98312 | tf_op jit(solution)/shard_map/ppermute | solution.py:27
  11.8 3.9 %collective-permute-start.3 = (f32[8,4,1,256]{3,2,1,0:T(1,128)S(1)}, f32[8,4,1,256]{3,2,1,0:T(1,128)S(1)}, u32[]{:S(2)}, u32[]{:S(2)}) collective-permute-start(f32[8,4,1,256]{3,2,1,0:T(1,128)S(1)} %get-tuple-element.246), channel_id=1, source_target_pairs={{2,0},{0,2},{3,1},{1,3},{6,4},{4,6},{7,5},{5,7},{10,8},{8,10},{11,... | collective-permute-start | bytes 98312 | tf_op jit(solution)/shard_map/ppermute | solution.py:29
  17.3 1.4 %collective-permute-start.4 = (f32[8,4,6,32]{3,2,1,0:T(8,128)S(1)}, f32[8,4,6,32]{3,2,1,0:T(8,128)S(1)}, u32[]{:S(2)}, u32[]{:S(2)}) collective-permute-start(f32[8,4,6,32]{3,2,1,0:T(8,128)S(1)} %get-tuple-element.204), channel_id=1, source_target_pairs={{0,1},{1,0},{2,3},{3,2},{4,5},{5,4},{6,7},{7,6},{8,9},{9,8},{10,11... | collective-permute-start | bytes 73736 | tf_op jit(solution)/shard_map/ppermute | solution.py:27
  17.4 1.5 %collective-permute-start.5 = (f32[8,4,6,32]{3,2,1,0:T(8,128)S(1)}, f32[8,4,6,32]{3,2,1,0:T(8,128)S(1)}, u32[]{:S(2)}, u32[]{:S(2)}) collective-permute-start(f32[8,4,6,32]{3,2,1,0:T(8,128)S(1)} %get-tuple-element.203), channel_id=1, source_target_pairs={{1,0},{0,1},{3,2},{2,3},{5,4},{4,5},{7,6},{6,7},{9,8},{8,9},{11,10... | collective-permute-start | bytes 73736 | tf_op jit(solution)/shard_map/ppermute | solution.py:29
  23.9 0.8 copy-start.3
  37.7 0.7 copy-start.6
  38.7 0.7 copy-start.7
  39.3 0.9 copy-start.4
  40.3 1.1 copy-start.1

commit v2 on v1

--- a/solution.py
+++ b/solution.py
@@ -15,48 +15,6 @@
 PRECISE = lax.Precision.HIGHEST
 KAPPAS = (0.12, 0.1)
 SLOPE_SHARE = 0.5
-
-
-def extended(cells, sides, width):
-    for axis, dim in sides:
-        count = lax.axis_size(axis)
-        head = lax.slice_in_dim(cells, 0, width, axis=dim)
-        tail = lax.slice_in_dim(cells, cells.shape[dim] - width, cells.shape[dim], axis=dim)
-        cells = jnp.concatenate(
-            [
-                lax.ppermute(tail, axis, [(i, (i + 1) % count) for i in range(count)]),
-                cells,
-                lax.ppermute(head, axis, [((i + 1) % count, i) for i in range(count)]),
-            ],
-            axis=dim,
-        )
-    return cells
-
-
-def along_rows(tensor, stride):
-    positions = jnp.arange(tensor.shape[-1]) % X_LEN
-    if stride > 0:
-        return jnp.where(
-            positions == X_LEN - 1,
-            jnp.roll(tensor, X_LEN - 1, axis=-1),
-            jnp.roll(tensor, -1, axis=-1),
-        )
-    return jnp.where(
-        positions == 0, jnp.roll(tensor, 1 - X_LEN, axis=-1), jnp.roll(tensor, 1, axis=-1)
-    )
-
-
-def region_view(tensor, shift_t, shift_z, shift_y):
-    span_t = tensor.shape[-3] - 2
-    span_z = tensor.shape[-2] - 2
-    span_yx = tensor.shape[-1] - 2 * X_LEN
-    start_y = (1 + shift_y) * X_LEN
-    return tensor[
-        ...,
-        1 + shift_t : 1 + shift_t + span_t,
-        1 + shift_z : 1 + shift_z + span_z,
-        start_y : start_y + span_yx,
-    ]
 
 
 def rotate_one(quadruple, theta_field):
@@ -115,75 +73,6 @@
             channels.append(jnp.cos(link_phase[direction]))
             channels.append(jnp.sin(link_phase[direction]))
     return jnp.stack(channels, axis=0)
-
-
-def tap_rows(padded, block_index):
-    shift_t = block_index // 9 - 1
-    shift_z = block_index // 3 % 3 - 1
-    shift_y = block_index % 3 - 1
-    centre = region_view(padded, shift_t, shift_z, shift_y)
-    return jnp.concatenate([along_rows(centre, -1), centre, along_rows(centre, 1)], axis=0)
-
-
-def conv_forward(padded, kernel, bias_hidden):
-    summed = None
-    for block_index in range(27):
-        rows_in = tap_rows(padded, block_index)
-        part_sum = jnp.einsum(
-            "ci,c...->i...",
-            kernel[24 * block_index : 24 * block_index + 24],
-            rows_in,
-            precision=PRECISE,
-        )
-        summed = part_sum if summed is None else summed + part_sum
-    return summed + bias_hidden[:, None, None, None]
-
-
-def coupling_forward(padded, time_angle, active_float, kernel, bias_hidden, readout, bias_out):
-    hidden = jnp.tanh(conv_forward(padded, kernel, bias_hidden))
-    squashed = jnp.tanh(
-        jnp.einsum("ik,i...->k...", readout, hidden, precision=PRECISE)
-        + bias_out[:, None, None, None]
-    )
-    coeffs = SLOPE_SHARE * 2.0 * math.pi / KNOTS * squashed
-    values, slopes = spline_basis(time_angle)
-    moved_angle = time_angle + active_float * jnp.sum(coeffs * values, axis=0)
-    jacobian = 1.0 + active_float * (KNOTS / (2.0 * math.pi)) * jnp.sum(coeffs * slopes, axis=0)
-    return (hidden, squashed, values, slopes, moved_angle, jacobian)
-
-
-def coupling_backward(
-    padded,
-    hidden,
-    squashed,
-    values,
-    slopes,
-    jacobian,
-    active_float,
-    force_field,
-    readout,
-    root_volume,
-):
-    ratio_const = KNOTS / (2.0 * math.pi)
-    scale_const = SLOPE_SHARE * 2.0 * math.pi / KNOTS
-    coeff_grad = (
-        active_float * (force_field * values - ratio_const * slopes / jacobian) / root_volume
-    )
-    logit_grad = coeff_grad * scale_const * (1.0 - squashed * squashed)
-    readout_part = jnp.einsum("i...,k...->ik", hidden, logit_grad, precision=PRECISE)
-    out_part = jnp.sum(logit_grad, axis=(1, 2, 3))
-    pre_grad = jnp.einsum("ik,k...->i...", readout, logit_grad, precision=PRECISE) * (
-        1.0 - hidden * hidden
-    )
-    hidden_part = jnp.sum(pre_grad, axis=(1, 2, 3))
-    kernel_part = jnp.concatenate(
-        [
-            jnp.einsum("c...,i...->ci", tap_rows(padded, block_index), pre_grad, precision=PRECISE)
-            for block_index in range(27)
-        ],
-        axis=0,
-    )
-    return (kernel_part, hidden_part, readout_part, out_part)
 
 
 GROUP = ("ta", "gz", "gy")
@@ -314,10 +203,12 @@
 
 
 def along_x(tensor, stride):
+    axis = tensor.ndim - 1
     place = lax.rem(lanes_of(tensor.shape), X_LEN)
+    wrap = X_LEN - 1
     if stride > 0:
-        return jnp.where(place == X_LEN - 1, turned(tensor, X_LEN - 1, 2), turned(tensor, -1, 2))
-    return jnp.where(place == 0, turned(tensor, 1 - X_LEN, 2), turned(tensor, 1, 2))
+        return jnp.where(place == wrap, turned(tensor, wrap, axis), turned(tensor, -1, axis))
+    return jnp.where(place == 0, turned(tensor, -wrap, axis), turned(tensor, 1, axis))
 
 
 def each_part():
@@ -698,11 +589,11 @@
     each(count - 1, lambda index: gather(index, lax.rem(mine + count - index - 1, count)).wait())
 
 
-def group_sum(arrays):
+def group_sum(table):
     count = group_size()
-    flat = jnp.concatenate([a.reshape(-1) for a in arrays])
-    chunk = -(-flat.size // (count * 1024)) * 8
-    data = jnp.pad(flat, (0, count * chunk * 128 - flat.size)).reshape((count * chunk, 128))
+    tiles = table.reshape((2, 8, 8, 128)).transpose((0, 2, 1, 3)).reshape((128, 128))
+    chunk = -(-16 // count) * 8
+    data = jnp.pad(tiles, ((0, count * chunk - 128), (0, 0)))
     dma = lambda *dims: pltpu.SemaphoreType.DMA(dims)
     summed = pl.pallas_call(
         sum_kernel,
@@ -720,45 +611,132 @@
         compiler_params=pltpu.CompilerParams(
             collective_id=1, has_side_effects=True, vmem_limit_bytes=32 * 1024 * 1024
         ),
-    )(data).reshape(-1)
-    results, start = [], 0
-    for a in arrays:
-        results.append(summed[start : start + a.size].reshape(a.shape))
-        start += a.size
-    return results
-
-
-def extend(tensor, margin):
-    face_ext = extended(tensor, (("ta", 1), ("gz", 2)), margin)
-    return extended(face_ext, (("gy", 3),), margin * X_LEN)
+    )(data)
+    return summed[:128].reshape((2, 8, 8, 128)).transpose((0, 2, 1, 3)).reshape((16, 1024))
+
+
+def tap_kernel(feature_ref, taps_ref, ext, ssem, rsem):
+    nt, nz, channels, width = feature_ref.shape
+    edge = 128
+    for t in range(nt):
+        for z in range(nz):
+            ext[1 + t, 1 + z, :, edge : edge + width] = feature_ref[t, z]
+    greet_group()
+
+    def swap(index, axis, low, low_halo, high, high_halo):
+        copies = []
+        for side, (src, dst) in enumerate(((low, high_halo), (high, low_halo))):
+            copies.append(
+                pltpu.make_async_remote_copy(
+                    src_ref=src,
+                    dst_ref=dst,
+                    send_sem=ssem.at[2 * index + side],
+                    recv_sem=rsem.at[2 * index + side],
+                    device_id=step_along(axis, 1 if side else -1),
+                    device_id_type=MESH,
+                )
+            )
+        for copy in copies:
+            copy.start()
+        for copy in copies:
+            copy.wait()
+
+    body = pl.ds(edge, width)
+    mid = pl.ds(1, nz)
+    swap(
+        0,
+        "ta",
+        ext.at[1, mid, :, body],
+        ext.at[0, mid, :, body],
+        ext.at[nt, mid, :, body],
+        ext.at[nt + 1, mid, :, body],
+    )
+    swap(
+        1,
+        "gz",
+        ext.at[:, 1, :, body],
+        ext.at[:, 0, :, body],
+        ext.at[:, nz, :, body],
+        ext.at[:, nz + 1, :, body],
+    )
+    swap(
+        2,
+        "gy",
+        ext.at[:, :, :, pl.ds(edge, edge)],
+        ext.at[:, :, :, pl.ds(0, edge)],
+        ext.at[:, :, :, pl.ds(width, edge)],
+        ext.at[:, :, :, pl.ds(edge + width, edge)],
+    )
+    for tt in range(nt + 2):
+        for zz in range(nz + 2):
+            cells = ext[tt, zz]
+            for oy in (-1, 0, 1):
+                base = turned(cells, -(edge + X_LEN * oy), 1)[:, 0:width]
+                for ox in (-1, 0, 1):
+                    tile = base if ox == 0 else along_x(base, ox)
+                    for ot in (-1, 0, 1):
+                        for oz in (-1, 0, 1):
+                            t, z = tt - 1 - ot, zz - 1 - oz
+                            if 0 <= t < nt and 0 <= z < nz:
+                                tap = 27 * (ot + 1) + 9 * (oz + 1) + 3 * (oy + 1) + ox + 1
+                                start = (t * nz + z) * width
+                                taps_ref[tap * channels : (tap + 1) * channels, start : start + width] = tile
+
+
+def conditioner_taps(features):
+    nt, nz, channels, width = features.shape
+    return pl.pallas_call(
+        tap_kernel,
+        out_shape=jax.ShapeDtypeStruct((81 * channels, nt * nz * width), F32),
+        in_specs=[pl.BlockSpec(memory_space=pltpu.VMEM)],
+        out_specs=pl.BlockSpec(memory_space=pltpu.VMEM),
+        scratch_shapes=[
+            pltpu.VMEM((nt + 2, nz + 2, channels, width + 256), F32),
+            pltpu.SemaphoreType.DMA((6,)),
+            pltpu.SemaphoreType.DMA((6,)),
+        ],
+        compiler_params=pltpu.CompilerParams(
+            collective_id=2, has_side_effects=True, vmem_limit_bytes=32 * 1024 * 1024
+        ),
+    )(features)
 
 
 def on_device(pseudo, frame_quat, link_phase, active, kernel, bias_hidden, readout, bias_out):
-    active_float = active.astype(jnp.float32)
-    padded_inputs = extend(conditioner_inputs(link_phase, active), 1)
-    hidden, squashed, values, slopes, moved_angle, jacobian = coupling_forward(
-        padded_inputs, link_phase[0], active_float, kernel, bias_hidden, readout, bias_out
+    scale = SLOPE_SHARE * 2.0 * math.pi / KNOTS
+    ratio = KNOTS / (2.0 * math.pi)
+    mask = active.astype(F32).reshape((-1,))
+    taps = conditioner_taps(conditioner_inputs(link_phase, active).transpose((1, 2, 0, 3)))
+    summed = jnp.einsum("ti,ts->is", kernel, taps, precision=lax.Precision.HIGH)
+    hidden = jnp.tanh(summed + bias_hidden[:, None])
+    logits = jnp.einsum("ik,is->ks", readout, hidden, precision=PRECISE)
+    squashed = jnp.tanh(logits + bias_out[:, None])
+    coeffs = scale * squashed
+    angle = link_phase[0].reshape((-1,))
+    values, slopes = spline_basis(angle)
+    moved = angle + mask * jnp.sum(coeffs * values, axis=0)
+    jacobian = 1.0 + mask * ratio * jnp.sum(coeffs * slopes, axis=0)
+    angles = jnp.concatenate([moved.reshape((1,) + active.shape), link_phase[1:]], axis=0)
+    solution, force_field = conjugate_gradient(pseudo, rotate_links(frame_quat, angles))
+    root_volume = math.sqrt(active.size * group_size())
+    force = force_field.reshape((-1,))
+    coeff_grad = mask * (force * values - ratio * slopes / jacobian) / root_volume
+    logit_grad = coeff_grad * scale * (1.0 - squashed * squashed)
+    pre_grad = jnp.einsum("ik,ks->is", readout, logit_grad, precision=PRECISE) * (1.0 - hidden * hidden)
+    kernel_part = jnp.einsum("is,ts->it", pre_grad, taps, precision=lax.Precision.HIGH)
+    readout_part = jnp.einsum("is,ks->ik", hidden, logit_grad, precision=PRECISE)
+    hidden_part = jnp.sum(pre_grad, axis=1, keepdims=True)
+    out_part = jnp.pad(jnp.sum(logit_grad, axis=1, keepdims=True), ((0, 16 - KNOTS), (0, 0)))
+    n = kernel.shape[0]
+    table = jnp.concatenate([kernel_part, readout_part, hidden_part, out_part], axis=1)
+    table = group_sum(jnp.pad(table, ((0, 0), (0, 1024 - table.shape[1]))))
+    return (
+        solution,
+        force_field,
+        table[:, :n].T,
+        table[:, n + KNOTS],
+        table[:, n : n + KNOTS],
+        table[:KNOTS, n + KNOTS + 1],
     )
-    angles = jnp.concatenate([moved_angle[None], link_phase[1:]], axis=0)
-    gauge_core = rotate_links(frame_quat, angles)
-    solution, force_field = conjugate_gradient(pseudo, gauge_core)
-    root_volume = math.sqrt(active.size * group_size())
-    kernel_part, hidden_part, readout_part, out_part = coupling_backward(
-        padded_inputs,
-        hidden,
-        squashed,
-        values,
-        slopes,
-        jacobian,
-        active_float,
-        force_field,
-        readout,
-        root_volume,
-    )
-    grad_kernel, grad_hidden, grad_readout, grad_out = group_sum(
-        (kernel_part, hidden_part, readout_part, out_part)
-    )
-    return (solution, force_field, grad_kernel, grad_hidden, grad_readout, grad_out)
 
 
 def solution(mesh):

time: 114 us -> 93.2 us (0.82)
  Pallas kernels: 56.4 us -> 72.4 us
  matrix products: 19 us -> 6.96 us
  starting transfers between devices: 7.83 us -> 0 us
  other arithmetic: 10.1 us -> 4.24 us
  waiting for transfers between devices: 5.5 us -> 0 us
  local copies, waits for them, and re-layouts: 13.4 us -> 8.01 us
    pallas_call x0 -> x1, Pallas kernels: none -> 16.6 us  [conditioner_taps(): pl.pallas_call(tap_kernel, out_shape=jax.ShapeDtypeStruct((81 * channels,...]
    dot_general x57 -> x5, matrix products: 19 us -> 6.96 us  [the longest x1 4.67 us: on_device(): jnp.einsum('is,ts->it', pre_grad, taps, precision=lax.Precision.HIGH)]
    ppermute x6 -> x0, starting transfers between devices: 7.83 us -> none  [the longest x3 4.7 us: extended(): lax.ppermute(tail, axis, [(i, (i + 1) % count) for i in range(count)])]
    ppermute x6 -> x0, waiting for transfers between devices: 5.5 us -> none  [the longest x3 3.58 us: extended(): lax.ppermute(tail, axis, [(i, (i + 1) % count) for i in range(count)])]
    select_n x14 -> x0, other arithmetic: 4.07 us -> none  [the longest x7 2.13 us: along_rows(): jnp.where(positions == 0, jnp.roll(tensor, 1 - X_LEN, axis=-1), jnp.roll(...]
    slice x23 -> x4, local copies, waits for them, and re-layouts: 6.35 us -> 2.31 us  [the longest x1 0.86 us: rotate_one(): quadruple[2]]
    concatenate x35 -> x1, other arithmetic: 2.7 us -> 0.08 us  [on_device(): jnp.concatenate([kernel_part, readout_part, hidden_part, out_part], axis=1)]
    unnamed x19 -> x3, other arithmetic: 2.89 us -> 0.77 us
  transfers between devices with their start and end apart: 6 -> 0, of which waited for: 6 -> 0; matrix products, arithmetic and copies ran while one was open for 1% -> 0% of each run, Pallas kernels for 0% -> 0%
where the time goes in v2:
time: 93.2 us; the launch traced here: 92.5 us
  Pallas kernels  72.4 us (78%)
  local copies, waits for them, and re-layouts  8.01 us (9%)
  matrix products  6.96 us (7%)
  other arithmetic  4.24 us (5%)
    pallas_call x1, Pallas kernels, conjugate_gradient(): pl.pallas_call(cg_kernel, out_shape=(jax.ShapeDtypeStruct((2, 4, 2, 2, nt...  42.8 us
    pallas_call x1, Pallas kernels, conditioner_taps(): pl.pallas_call(tap_kernel, out_shape=jax.ShapeDtypeStruct((81 * channels,...  16.6 us
    pallas_call x1, Pallas kernels, group_sum(): pl.pallas_call(sum_kernel, out_shape=jax.ShapeDtypeStruct(data.shape, F32...  13 us
    dot_general x1, matrix products, on_device(): jnp.einsum('is,ts->it', pre_grad, taps, precision=lax.Precision.HIGH)  4.67 us
    unnamed x21, local copies, waits for them, and re-layouts  4.34 us

profile of v2, /device:TPU:0, one launch (start us, length us, event | category | flops | bytes accessed | tf_op | source)
XLA Modules:
  0.0 92.5 jit_solution(9688768830392500994)
XLA Ops:
  0.6 0.0 copy-start
  0.6 0.0 copy-start.5
  0.7 0.9 fusion.28
  1.5 0.8 multiply_bitcast_fusion.1
  2.3 0.5 multiply_add_fusion.1
  2.8 0.3 multiply_add_fusion.5
  3.1 0.8 fusion.22
  3.9 0.1 stack.16
  4.0 0.0 copy-start.4
  4.0 0.0 copy-start.6
  4.0 0.0 copy-start.3
  4.0 0.0 copy-start.2
  4.1 16.6 %shard_map.127 = f32[648,2048]{1,0:T(8,128)S(1)} custom-call(f32[2,4,8,256]{3,2,1,0:T(8,128)S(1)} %bitcast.114), custom_call_target="tpu_custom_call" | custom-call | tf_op jit(solution)/shard_map/pallas_call | solution.py:688
  20.7 0.0 copy-start.1
  20.7 2.3 %copy-done.1 = f32[648,2048]{1,0:T(8,128)} copy-done((f32[648,2048]{1,0:T(8,128)}, f32[648,2048]{1,0:T(8,128)S(1)}, u32[]{:S(2)}) %copy-start.1) | copy-done | bytes 5308440
  23.0 0.0 copy-done
  23.0 0.0 copy-done.5
  23.0 1.4 %fusion = f32[2048,16]{0,1:T(8,128)S(1)} fusion(f32[648,2048]{1,0:T(8,128)S(1)} %shard_map.127, f32[648,16]{0,1:T(8,128)S(1)} %copy-done, f32[16]{0:T(128)S(1)} %copy-done.5), kind=kOutput, calls=%fused_computation.2 | convolution fusion | flops 127434752 | bytes 5481024 | tf_op jit(solution)/shard_map/ti,ts->is/dot_general | solution.py:709
  24.4 0.0 copy-done.4
  24.4 0.0 copy-done.6
  24.4 0.3 fusion.7
  24.7 0.0 copy-done.3
  24.7 0.8 fusion.14
  25.5 0.8 fusion.13
  26.3 0.2 concatenate.6
  26.6 0.1 copy.112
  26.7 0.0 copy-done.2
  26.7 42.8 %shard_map.128 = (f32[2,4,2,2,2,4,256]{6,5,4,3,2,1,0:T(4,128)S(1)}, f32[2,4,256]{2,1,0:T(4,128)S(1)}) custom-call(f32[2,4,2,2,2,4,256]{6,5,4,3,2,1,0:T(4,128)S(1)} %bitcast.115, f32[4,4,2,4,256]{4,3,2,1,0:T(4,128)S(1)} %bitcast.113), custom_call_target="tpu_custom_call" | custom-call | tf_op jit(solution)/shard_map/pallas_call | solution.py:512
  69.5 0.2 fusion.25
  69.8 0.4 fusion.29
  70.2 4.7 %fusion.30 = f32[16,648]{1,0:T(8,128)S(1)} fusion(f32[2048,16]{0,1:T(8,128)S(1)} %get-tuple-element.88, f32[648,2048]{1,0:T(8,128)} %copy-done.1), kind=kOutput, calls=%fused_computation.83 | convolution fusion | flops 127401984 | bytes 5480960 | tf_op jit(solution)/shard_map/is,ts->it/dot_general | solution.py:725
  74.9 0.2 fusion.31
  75.1 0.1 copy.115
  75.2 0.1 copy.113
  75.3 0.1 select_maximum_fusion
  75.4 0.1 pad.9
  75.4 13.0 %shard_map.129 = f32[128,128]{1,0:T(8,128)S(1)} custom-call(f32[128,128]{1,0:T(8,128)S(1)} %bitcast.116), custom_call_target="tpu_custom_call" | custom-call | tf_op jit(solution)/shard_map/pallas_call | solution.py:598
  88.5 0.6 slice_bitcast_fusion
  89.1 0.1 slice.146
  89.2 0.7 copy.117
  89.8 0.7 slice_reduce_fusion
  90.5 0.7 slice_reduce_fusion.1
  91.2 0.7 copy.222
  91.9 0.6 copy.223
  (15 shorter events, 0.1 us)
Async XLA Ops:
  0.6 22.4 %copy-start = (f32[648,16]{0,1:T(8,128)S(1)}, f32[648,16]{0,1:T(8,128)}, u32[]{:S(2)}) copy-start(f32[648,16]{0,1:T(8,128)} %param.12) | copy-start | bytes 124420
  0.6 22.4 %copy-start.5 = (f32[16]{0:T(128)S(1)}, f32[16]{0:T(128)}, u32[]{:S(2)}) copy-start(f32[16]{0:T(128)} %param.13) | copy-start | bytes 196
  4.0 20.4 %copy-start.4 = (f32[16,8]{0,1:T(8,128)S(1)}, f32[16,8]{0,1:T(8,128)}, u32[]{:S(2)}) copy-start(f32[16,8]{0,1:T(8,128)} %param.14) | copy-start | bytes 1540
  4.0 20.4 %copy-start.6 = (f32[8]{0:T(128)S(1)}, f32[8]{0:T(128)}, u32[]{:S(2)}) copy-start(f32[8]{0:T(128)} %param.15) | copy-start | bytes 100
  4.0 20.7 %copy-start.3 = (s32[2,4,256]{2,1,0:T(4,128)S(1)}, s32[2,4,256]{2,1,0:T(4,128)}, u32[]{:S(2)}) copy-start(s32[2,4,256]{2,1,0:T(4,128)} %param.11) | copy-start | bytes 24580
  4.0 22.6 %copy-start.2 = (f32[32,2,4,256]{3,2,1,0:T(4,128)S(1)}, f32[32,2,4,256]{3,2,1,0:T(4,128)}, u32[]{:S(2)}) copy-start(f32[32,2,4,256]{3,2,1,0:T(4,128)} %param.8) | copy-start | bytes 786436
  20.7 2.3 %copy-start.1 = (f32[648,2048]{1,0:T(8,128)}, f32[648,2048]{1,0:T(8,128)S(1)}, u32[]{:S(2)}) copy-start(f32[648,2048]{1,0:T(8,128)S(1)} %shard_map.127) | copy-start | bytes 15925252

commit v3 on v2

--- a/solution.py
+++ b/solution.py
@@ -105,27 +105,34 @@
         lax.fori_loop(0, count, looped, 0)
 
 
-def peer(offset):
-    nz, ny = lax.axis_size("gz"), lax.axis_size("gy")
-    mine = (lax.axis_index("ta") * nz + lax.axis_index("gz")) * ny + lax.axis_index("gy")
-    target = lax.rem(mine + offset, group_size())
-    return {
-        "groups": lax.axis_index("groups"),
-        "ta": target // (nz * ny),
-        "gz": lax.rem(target // ny, nz),
-        "gy": lax.rem(target, ny),
-    }
-
-
-def greet_group():
+def plane_size():
+    return lax.axis_size("gz") * lax.axis_size("gy")
+
+
+def plane_place():
+    return lax.axis_index("gz") * lax.axis_size("gy") + lax.axis_index("gy")
+
+
+def plane_peer(offset):
+    ny = lax.axis_size("gy")
+    target = lax.rem(plane_place() + offset, plane_size())
+    return {"gz": target // ny, "gy": lax.rem(target, ny)}
+
+
+def time_peer(offset):
+    return {"ta": lax.rem(lax.axis_index("ta") + offset, lax.axis_size("ta"))}
+
+
+def greet_lines():
     barrier = pltpu.get_barrier_semaphore()
-    count = group_size() - 1
-
-    def greet(index):
-        pl.semaphore_signal(barrier, inc=1, device_id=peer(index + 1), device_id_type=MESH)
-
-    each(count, greet)
-    pl.semaphore_wait(barrier, count)
+    planes, times = plane_size() - 1, lax.axis_size("ta") - 1
+    for count, partner in ((planes, plane_peer), (times, time_peer)):
+
+        def greet(index):
+            pl.semaphore_signal(barrier, inc=1, device_id=partner(index + 1), device_id_type=MESH)
+
+        each(count, greet)
+    pl.semaphore_wait(barrier, planes + times)
 
 
 def step_along(axis, distance):
@@ -238,16 +245,20 @@
     ratio,
     red_send,
     red_recv,
+    line_send,
+    line_recv,
     halo_ssem,
     halo_rsem,
     f_ssem,
     f_rsem,
     red_ssem,
     red_rsem,
+    line_ssem,
+    line_rsem,
 ):
     nt, nz, width = pseudo_ref.shape[-3:]
     shape = (2, nt * nz, width)
-    others = group_size() - 1
+    planes, times = plane_size() - 1, lax.axis_size("ta") - 1
     row, lane = rows_of(shape), lanes_of(shape)
     z_place = lax.rem(row, nz)
     t_low = row < (nt - 1) * nz
@@ -276,7 +287,7 @@
         out[s] = zero
     ratio[...] = jnp.ones(ratio.shape, F32)
 
-    greet_group()
+    greet_lines()
 
     def reduce_copy(parity, index):
         return pltpu.make_async_remote_copy(
@@ -284,7 +295,17 @@
             dst_ref=red_recv.at[parity, index],
             send_sem=red_ssem.at[parity, index],
             recv_sem=red_rsem.at[parity, index],
-            device_id=peer(index + 1),
+            device_id=plane_peer(index + 1),
+            device_id_type=MESH,
+        )
+
+    def line_copy(parity, index):
+        return pltpu.make_async_remote_copy(
+            src_ref=line_send.at[parity],
+            dst_ref=line_recv.at[parity, index],
+            send_sem=line_ssem.at[parity, index],
+            recv_sem=line_rsem.at[parity, index],
+            device_id=time_peer(index + 1),
             device_id_type=MESH,
         )
 
@@ -295,11 +316,16 @@
         sums = jnp.sum(folded, axis=1, keepdims=True)
         tile_row = rows_of((8, 128))
         red_send[parity] = jnp.where(tile_row == 0, sums[0], jnp.where(tile_row == 1, sums[1], 0.0))
-        each(others, lambda index: reduce_copy(parity, index).start())
+        each(planes, lambda index: reduce_copy(parity, index).start())
+
+    def pass_sum(parity):
+        each(planes, lambda index: reduce_copy(parity, index).wait())
+        line_send[parity] = red_send[parity] + jnp.sum(red_recv[parity], axis=0)
+        each(times, lambda index: line_copy(parity, index).start())
 
     def finish_sum(parity):
-        each(others, lambda index: reduce_copy(parity, index).wait())
-        total = red_send[parity] + jnp.sum(red_recv[parity], axis=0)
+        each(times, lambda index: line_copy(parity, index).wait())
+        total = line_send[parity] + jnp.sum(line_recv[parity], axis=0)
         total = jnp.broadcast_to(jnp.sum(total, axis=1, keepdims=True), (8, 128))
         return jnp.where(rows_of((8, 128)) < 2, total, 1.0)
 
@@ -396,6 +422,7 @@
             for c in range(2):
                 for r in range(2):
                     out[s, c, r] = total[s][c][r]
+        pass_sum(parity)
         for mu in (2, 1, 0):
             total = [[[out[s, c, r] for r in range(2)] for c in range(2)] for s in range(4)]
             for back in range(2):
@@ -453,6 +480,10 @@
         def _():
             turned_wilson(1, 1)
 
+        @pl.when(k == ITERS - 1)
+        def _():
+            pass_sum(1)
+
         length = spread(ratio[...] / finish_sum(1))
         for s in range(4):
             xs[s] = xs[s] + length * dvec[s]
@@ -505,7 +536,7 @@
 def conjugate_gradient(pseudo, gauge):
     nt, nz, width = pseudo.shape[1:]
     rows = nt * nz
-    others = group_size() - 1
+    planes, times = plane_size() - 1, lax.axis_size("ta") - 1
     field = (4, 2, 2, 2, rows, width)
     vmem = lambda *dims: pltpu.VMEM(dims, F32)
     dma = lambda *dims: pltpu.SemaphoreType.DMA(dims)
@@ -535,13 +566,17 @@
             vmem(2, 4, 2, rows, width),
             vmem(8, 128),
             vmem(2, 8, 128),
-            vmem(2, others, 8, 128),
+            vmem(2, planes, 8, 128),
+            vmem(2, 8, 128),
+            vmem(2, times, 8, 128),
             dma(6),
             dma(2, 6),
             dma(2),
             dma(2),
-            dma(2, others),
-            dma(2, others),
+            dma(2, planes),
+            dma(2, planes),
+            dma(2, times),
+            dma(2, times),
         ],
         compiler_params=pltpu.CompilerParams(
             collective_id=0, has_side_effects=True, vmem_limit_bytes=32 * 1024 * 1024
@@ -550,63 +585,65 @@
     return sol.reshape(pseudo.shape), force
 
 
-def sum_kernel(data_ref, out_ref, landed, reduced, ssem, rsem, gather_ssem, gather_rsem):
-    count = group_size()
-    chunk = data_ref.shape[0] // count
-    nz, ny = lax.axis_size("gz"), lax.axis_size("gy")
-    mine = (lax.axis_index("ta") * nz + lax.axis_index("gz")) * ny + lax.axis_index("gy")
-    greet_group()
+def sum_kernel(data_ref, out_ref, landed, lined, reduced, *sems):
+    planes, times = plane_size(), lax.axis_size("ta")
+    chunk = data_ref.shape[0] // planes
+    place, now = plane_place(), lax.axis_index("ta")
+    greet_lines()
 
     def part_of(device):
         return pl.ds(pl.multiple_of(device * chunk, 8), chunk)
 
-    def scatter(index):
+    def copy(stage, index, src, dst, target):
         return pltpu.make_async_remote_copy(
-            src_ref=data_ref.at[part_of(lax.rem(mine + index + 1, count))],
-            dst_ref=landed.at[index],
-            send_sem=ssem.at[index],
-            recv_sem=rsem.at[index],
-            device_id=peer(index + 1),
+            src_ref=src,
+            dst_ref=dst,
+            send_sem=sems[2 * stage].at[index],
+            recv_sem=sems[2 * stage + 1].at[index],
+            device_id=target,
             device_id_type=MESH,
         )
 
+    def scatter(index):
+        src = data_ref.at[part_of(lax.rem(place + index + 1, planes))]
+        return copy(0, index, src, landed.at[index], plane_peer(index + 1))
+
+    def across(index, owner):
+        return copy(1, index, reduced.at[0], lined.at[owner], time_peer(index + 1))
+
     def gather(index, owner):
-        return pltpu.make_async_remote_copy(
-            src_ref=reduced,
-            dst_ref=out_ref.at[part_of(owner)],
-            send_sem=gather_ssem.at[index],
-            recv_sem=gather_rsem.at[index],
-            device_id=peer(index + 1),
-            device_id_type=MESH,
-        )
-
-    each(count - 1, lambda index: scatter(index).start())
-    each(count - 1, lambda index: scatter(index).wait())
-    total = data_ref[part_of(mine)] + jnp.sum(landed[...], axis=0)
-    reduced[...] = total
-    each(count - 1, lambda index: gather(index, mine).start())
-    out_ref[part_of(mine)] = total
-    each(count - 1, lambda index: gather(index, lax.rem(mine + count - index - 1, count)).wait())
+        return copy(2, index, reduced.at[1], out_ref.at[part_of(owner)], plane_peer(index + 1))
+
+    each(planes - 1, lambda index: scatter(index).start())
+    each(planes - 1, lambda index: scatter(index).wait())
+    partial = data_ref[part_of(place)] + jnp.sum(landed[...], axis=0)
+    reduced[0] = partial
+    each(times - 1, lambda index: across(index, now).start())
+    lined[now] = partial
+    each(times - 1, lambda index: across(index, lax.rem(now + times - index - 1, times)).wait())
+    total = jnp.sum(lined[...], axis=0)
+    reduced[1] = total
+    each(planes - 1, lambda index: gather(index, place).start())
+    out_ref[part_of(place)] = total
+    each(planes - 1, lambda index: gather(index, lax.rem(place + planes - index - 1, planes)).wait())
 
 
 def group_sum(table):
-    count = group_size()
+    planes, times = plane_size(), lax.axis_size("ta")
     tiles = table.reshape((2, 8, 8, 128)).transpose((0, 2, 1, 3)).reshape((128, 128))
-    chunk = -(-16 // count) * 8
-    data = jnp.pad(tiles, ((0, count * chunk - 128), (0, 0)))
-    dma = lambda *dims: pltpu.SemaphoreType.DMA(dims)
+    chunk = -(-16 // planes) * 8
+    data = jnp.pad(tiles, ((0, planes * chunk - 128), (0, 0)))
+    counts = (planes - 1, planes - 1, times - 1, times - 1, planes - 1, planes - 1)
     summed = pl.pallas_call(
         sum_kernel,
         out_shape=jax.ShapeDtypeStruct(data.shape, F32),
         in_specs=[pl.BlockSpec(memory_space=pltpu.VMEM)],
         out_specs=pl.BlockSpec(memory_space=pltpu.VMEM),
         scratch_shapes=[
-            pltpu.VMEM((count - 1, chunk, 128), F32),
-            pltpu.VMEM((chunk, 128), F32),
-            dma(count - 1),
-            dma(count - 1),
-            dma(count - 1),
-            dma(count - 1),
+            pltpu.VMEM((planes - 1, chunk, 128), F32),
+            pltpu.VMEM((times, chunk, 128), F32),
+            pltpu.VMEM((2, chunk, 128), F32),
+            *[pltpu.SemaphoreType.DMA((count,)) for count in counts],
         ],
         compiler_params=pltpu.CompilerParams(
             collective_id=1, has_side_effects=True, vmem_limit_bytes=32 * 1024 * 1024
@@ -621,7 +658,7 @@
     for t in range(nt):
         for z in range(nz):
             ext[1 + t, 1 + z, :, edge : edge + width] = feature_ref[t, z]
-    greet_group()
+    greet_lines()
 
     def swap(index, axis, low, low_halo, high, high_halo):
         copies = []

time: 93.2 us -> 94 us (level)
    pallas_call x1, Pallas kernels: 42.8 us -> 45.1 us  [conjugate_gradient(): pl.pallas_call(cg_kernel, out_shape=(jax.ShapeDtypeStruct((2, 4, 2, 2, nt...]
    pallas_call x1, Pallas kernels: 13 us -> 11.7 us  [group_sum(): pl.pallas_call(sum_kernel, out_shape=jax.ShapeDtypeStruct(data.shape, F32...]
where the time goes in v3:
time: 94 us; the launch traced here: 93.4 us
  Pallas kernels  73.3 us (78%)
  local copies, waits for them, and re-layouts  8.01 us (9%)
  matrix products  6.96 us (7%)
  other arithmetic  4.24 us (5%)
    pallas_call x1, Pallas kernels, conjugate_gradient(): pl.pallas_call(cg_kernel, out_shape=(jax.ShapeDtypeStruct((2, 4, 2, 2, nt...  45.1 us
    pallas_call x1, Pallas kernels, conditioner_taps(): pl.pallas_call(tap_kernel, out_shape=jax.ShapeDtypeStruct((81 * channels,...  16.5 us
    pallas_call x1, Pallas kernels, group_sum(): pl.pallas_call(sum_kernel, out_shape=jax.ShapeDtypeStruct(data.shape, F32...  11.7 us
    dot_general x1, matrix products, on_device(): jnp.einsum('is,ts->it', pre_grad, taps, precision=lax.Precision.HIGH)  4.67 us
    unnamed x21, local copies, waits for them, and re-layouts  4.34 us

profile of v3, /device:TPU:0, one launch (start us, length us, event | category | flops | bytes accessed | tf_op | source)
XLA Modules:
  0.0 93.4 jit_solution(7440177783519690683)
XLA Ops:
  0.6 0.0 copy-start
  0.6 0.0 copy-start.5
  0.7 0.9 fusion.28
  1.5 0.8 multiply_bitcast_fusion.1
  2.3 0.5 multiply_add_fusion.1
  2.8 0.3 multiply_add_fusion.5
  3.1 0.8 fusion.22
  3.9 0.1 stack.16
  4.0 0.0 copy-start.4
  4.0 0.0 copy-start.6
  4.0 0.0 copy-start.3
  4.0 0.0 copy-start.2
  4.1 16.5 %shard_map.127 = f32[648,2048]{1,0:T(8,128)S(1)} custom-call(f32[2,4,8,256]{3,2,1,0:T(8,128)S(1)} %bitcast.114), custom_call_target="tpu_custom_call" | custom-call | tf_op jit(solution)/shard_map/pallas_call | solution.py:725
  20.6 0.0 copy-start.1
  20.6 2.3 %copy-done.1 = f32[648,2048]{1,0:T(8,128)} copy-done((f32[648,2048]{1,0:T(8,128)}, f32[648,2048]{1,0:T(8,128)S(1)}, u32[]{:S(2)}) %copy-start.1) | copy-done | bytes 5308440
  22.9 0.0 copy-done
  22.9 0.0 copy-done.5
  22.9 1.4 %fusion = f32[2048,16]{0,1:T(8,128)S(1)} fusion(f32[648,2048]{1,0:T(8,128)S(1)} %shard_map.127, f32[648,16]{0,1:T(8,128)S(1)} %copy-done, f32[16]{0:T(128)S(1)} %copy-done.5), kind=kOutput, calls=%fused_computation.2 | convolution fusion | flops 127434752 | bytes 5481024 | tf_op jit(solution)/shard_map/ti,ts->is/dot_general | solution.py:746
  24.3 0.0 copy-done.4
  24.3 0.0 copy-done.6
  24.3 0.3 fusion.7
  24.6 0.0 copy-done.3
  24.6 0.8 fusion.14
  25.4 0.8 fusion.13
  26.2 0.2 concatenate.6
  26.4 0.1 copy.112
  26.5 0.0 copy-done.2
  26.5 45.1 %shard_map.128 = (f32[2,4,2,2,2,4,256]{6,5,4,3,2,1,0:T(4,128)S(1)}, f32[2,4,256]{2,1,0:T(4,128)S(1)}) custom-call(f32[2,4,2,2,2,4,256]{6,5,4,3,2,1,0:T(4,128)S(1)} %bitcast.115, f32[4,4,2,4,256]{4,3,2,1,0:T(4,128)S(1)} %bitcast.113), custom_call_target="tpu_custom_call" | custom-call | tf_op jit(solution)/shard_map/pallas_call | solution.py:543
  71.7 0.2 fusion.25
  71.9 0.4 fusion.29
  72.3 4.7 %fusion.30 = f32[16,648]{1,0:T(8,128)S(1)} fusion(f32[2048,16]{0,1:T(8,128)S(1)} %get-tuple-element.88, f32[648,2048]{1,0:T(8,128)} %copy-done.1), kind=kOutput, calls=%fused_computation.83 | convolution fusion | flops 127401984 | bytes 5480960 | tf_op jit(solution)/shard_map/is,ts->it/dot_general | solution.py:762
  77.0 0.2 fusion.31
  77.3 0.1 copy.115
  77.4 0.1 copy.113
  77.4 0.1 select_maximum_fusion
  77.5 0.1 pad.9
  77.6 11.7 %shard_map.129 = f32[128,128]{1,0:T(8,128)S(1)} custom-call(f32[128,128]{1,0:T(8,128)S(1)} %bitcast.116), custom_call_target="tpu_custom_call" | custom-call | tf_op jit(solution)/shard_map/pallas_call | solution.py:637
  89.4 0.6 slice_bitcast_fusion
  90.0 0.1 slice.146
  90.1 0.7 copy.117
  90.7 0.7 slice_reduce_fusion
  91.4 0.7 slice_reduce_fusion.1
  92.1 0.7 copy.222
  92.8 0.6 copy.223
  (15 shorter events, 0.1 us)
Async XLA Ops:
  0.6 22.3 %copy-start = (f32[648,16]{0,1:T(8,128)S(1)}, f32[648,16]{0,1:T(8,128)}, u32[]{:S(2)}) copy-start(f32[648,16]{0,1:T(8,128)} %param.12) | copy-start | bytes 124420
  0.6 22.2 %copy-start.5 = (f32[16]{0:T(128)S(1)}, f32[16]{0:T(128)}, u32[]{:S(2)}) copy-start(f32[16]{0:T(128)} %param.13) | copy-start | bytes 196
  4.0 20.3 %copy-start.4 = (f32[16,8]{0,1:T(8,128)S(1)}, f32[16,8]{0,1:T(8,128)}, u32[]{:S(2)}) copy-start(f32[16,8]{0,1:T(8,128)} %param.14) | copy-start | bytes 1540
  4.0 20.3 %copy-start.6 = (f32[8]{0:T(128)S(1)}, f32[8]{0:T(128)}, u32[]{:S(2)}) copy-start(f32[8]{0:T(128)} %param.15) | copy-start | bytes 100
  4.0 20.5 %copy-start.3 = (s32[2,4,256]{2,1,0:T(4,128)S(1)}, s32[2,4,256]{2,1,0:T(4,128)}, u32[]{:S(2)}) copy-start(s32[2,4,256]{2,1,0:T(4,128)} %param.11) | copy-start | bytes 24580
  4.0 22.5 %copy-start.2 = (f32[32,2,4,256]{3,2,1,0:T(4,128)S(1)}, f32[32,2,4,256]{3,2,1,0:T(4,128)}, u32[]{:S(2)}) copy-start(f32[32,2,4,256]{3,2,1,0:T(4,128)} %param.8) | copy-start | bytes 786436
  20.6 2.3 %copy-start.1 = (f32[648,2048]{1,0:T(8,128)}, f32[648,2048]{1,0:T(8,128)S(1)}, u32[]{:S(2)}) copy-start(f32[648,2048]{1,0:T(8,128)S(1)} %shard_map.127) | copy-start | bytes 15925252

commit v4 on v3

--- a/solution.py
+++ b/solution.py
@@ -103,6 +103,31 @@
             return carry
 
         lax.fori_loop(0, count, looped, 0)
+
+
+def peer(offset):
+    nz, ny = lax.axis_size("gz"), lax.axis_size("gy")
+    mine = (lax.axis_index("ta") * nz + lax.axis_index("gz")) * ny + lax.axis_index("gy")
+    target = lax.rem(mine + offset, group_size())
+    return {
+        "groups": lax.axis_index("groups"),
+        "ta": target // (nz * ny),
+        "gz": lax.rem(target // ny, nz),
+        "gy": lax.rem(target, ny),
+    }
+
+
+def greet_group():
+    barrier = pltpu.get_barrier_semaphore()
+
+    def greet(index):
+        pl.semaphore_signal(barrier, inc=1, device_id=peer(index + 1), device_id_type=MESH)
+
+    each(group_size() - 1, greet)
+
+
+def await_group():
+    pl.semaphore_wait(pltpu.get_barrier_semaphore(), group_size() - 1)
 
 
 def plane_size():
@@ -245,20 +270,17 @@
     ratio,
     red_send,
     red_recv,
-    line_send,
-    line_recv,
     halo_ssem,
     halo_rsem,
     f_ssem,
     f_rsem,
     red_ssem,
     red_rsem,
-    line_ssem,
-    line_rsem,
 ):
+    greet_group()
     nt, nz, width = pseudo_ref.shape[-3:]
     shape = (2, nt * nz, width)
-    planes, times = plane_size() - 1, lax.axis_size("ta") - 1
+    others = group_size() - 1
     row, lane = rows_of(shape), lanes_of(shape)
     z_place = lax.rem(row, nz)
     t_low = row < (nt - 1) * nz
@@ -287,7 +309,7 @@
         out[s] = zero
     ratio[...] = jnp.ones(ratio.shape, F32)
 
-    greet_lines()
+    await_group()
 
     def reduce_copy(parity, index):
         return pltpu.make_async_remote_copy(
@@ -295,17 +317,7 @@
             dst_ref=red_recv.at[parity, index],
             send_sem=red_ssem.at[parity, index],
             recv_sem=red_rsem.at[parity, index],
-            device_id=plane_peer(index + 1),
-            device_id_type=MESH,
-        )
-
-    def line_copy(parity, index):
-        return pltpu.make_async_remote_copy(
-            src_ref=line_send.at[parity],
-            dst_ref=line_recv.at[parity, index],
-            send_sem=line_ssem.at[parity, index],
-            recv_sem=line_rsem.at[parity, index],
-            device_id=time_peer(index + 1),
+            device_id=peer(index + 1),
             device_id_type=MESH,
         )
 
@@ -316,16 +328,11 @@
         sums = jnp.sum(folded, axis=1, keepdims=True)
         tile_row = rows_of((8, 128))
         red_send[parity] = jnp.where(tile_row == 0, sums[0], jnp.where(tile_row == 1, sums[1], 0.0))
-        each(planes, lambda index: reduce_copy(parity, index).start())
-
-    def pass_sum(parity):
-        each(planes, lambda index: reduce_copy(parity, index).wait())
-        line_send[parity] = red_send[parity] + jnp.sum(red_recv[parity], axis=0)
-        each(times, lambda index: line_copy(parity, index).start())
+        each(others, lambda index: reduce_copy(parity, index).start())
 
     def finish_sum(parity):
-        each(times, lambda index: line_copy(parity, index).wait())
-        total = line_send[parity] + jnp.sum(line_recv[parity], axis=0)
+        each(others, lambda index: reduce_copy(parity, index).wait())
+        total = red_send[parity] + jnp.sum(red_recv[parity], axis=0)
         total = jnp.broadcast_to(jnp.sum(total, axis=1, keepdims=True), (8, 128))
         return jnp.where(rows_of((8, 128)) < 2, total, 1.0)
 
@@ -422,7 +429,6 @@
             for c in range(2):
                 for r in range(2):
                     out[s, c, r] = total[s][c][r]
-        pass_sum(parity)
         for mu in (2, 1, 0):
             total = [[[out[s, c, r] for r in range(2)] for c in range(2)] for s in range(4)]
             for back in range(2):
@@ -480,10 +486,6 @@
         def _():
             turned_wilson(1, 1)
 
-        @pl.when(k == ITERS - 1)
-        def _():
-            pass_sum(1)
-
         length = spread(ratio[...] / finish_sum(1))
         for s in range(4):
             xs[s] = xs[s] + length * dvec[s]
@@ -536,7 +538,7 @@
 def conjugate_gradient(pseudo, gauge):
     nt, nz, width = pseudo.shape[1:]
     rows = nt * nz
-    planes, times = plane_size() - 1, lax.axis_size("ta") - 1
+    others = group_size() - 1
     field = (4, 2, 2, 2, rows, width)
     vmem = lambda *dims: pltpu.VMEM(dims, F32)
     dma = lambda *dims: pltpu.SemaphoreType.DMA(dims)
@@ -566,17 +568,13 @@
             vmem(2, 4, 2, rows, width),
             vmem(8, 128),
             vmem(2, 8, 128),
-            vmem(2, planes, 8, 128),
-            vmem(2, 8, 128),
-            vmem(2, times, 8, 128),
+            vmem(2, others, 8, 128),
             dma(6),
             dma(2, 6),
             dma(2),
             dma(2),
-            dma(2, planes),
-            dma(2, planes),
-            dma(2, times),
-            dma(2, times),
+            dma(2, others),
+            dma(2, others),
         ],
         compiler_params=pltpu.CompilerParams(
             collective_id=0, has_side_effects=True, vmem_limit_bytes=32 * 1024 * 1024

time: 94 us -> 92.4 us (0.983)
  Pallas kernels: 73.3 us -> 71.7 us
    pallas_call x1, Pallas kernels: 45.1 us -> 43.6 us  [conjugate_gradient(): pl.pallas_call(cg_kernel, out_shape=(jax.ShapeDtypeStruct((2, 4, 2, 2, nt...]
where the time goes in v4:
time: 92.4 us; the launch traced here: 91.8 us
  Pallas kernels  71.7 us (78%)
  local copies, waits for them, and re-layouts  8.01 us (9%)
  matrix products  6.97 us (8%)
  other arithmetic  4.24 us (5%)
    pallas_call x1, Pallas kernels, conjugate_gradient(): pl.pallas_call(cg_kernel, out_shape=(jax.ShapeDtypeStruct((2, 4, 2, 2, nt...  43.6 us
    pallas_call x1, Pallas kernels, conditioner_taps(): pl.pallas_call(tap_kernel, out_shape=jax.ShapeDtypeStruct((81 * channels,...  16.5 us
    pallas_call x1, Pallas kernels, group_sum(): pl.pallas_call(sum_kernel, out_shape=jax.ShapeDtypeStruct(data.shape, F32...  11.6 us
    dot_general x1, matrix products, on_device(): jnp.einsum('is,ts->it', pre_grad, taps, precision=lax.Precision.HIGH)  4.67 us
    unnamed x21, local copies, waits for them, and re-layouts  4.34 us

profile of v4, /device:TPU:0, one launch (start us, length us, event | category | flops | bytes accessed | tf_op | source)
XLA Modules:
  0.0 91.8 jit_solution(1474299597526615064)
XLA Ops:
  0.6 0.0 copy-start
  0.6 0.0 copy-start.5
  0.7 0.9 fusion.28
  1.5 0.8 multiply_bitcast_fusion.1
  2.3 0.5 multiply_add_fusion.1
  2.8 0.3 multiply_add_fusion.5
  3.1 0.8 fusion.22
  3.9 0.1 stack.16
  4.0 0.0 copy-start.4
  4.0 0.0 copy-start.6
  4.0 0.0 copy-start.3
  4.0 0.0 copy-start.2
  4.1 16.5 %shard_map.127 = f32[648,2048]{1,0:T(8,128)S(1)} custom-call(f32[2,4,8,256]{3,2,1,0:T(8,128)S(1)} %bitcast.114), custom_call_target="tpu_custom_call" | custom-call | tf_op jit(solution)/shard_map/pallas_call | solution.py:723
  20.6 0.0 copy-start.1
  20.6 2.3 %copy-done.1 = f32[648,2048]{1,0:T(8,128)} copy-done((f32[648,2048]{1,0:T(8,128)}, f32[648,2048]{1,0:T(8,128)S(1)}, u32[]{:S(2)}) %copy-start.1) | copy-done | bytes 5308440
  22.9 0.0 copy-done
  22.9 0.0 copy-done.5
  22.9 1.4 %fusion = f32[2048,16]{0,1:T(8,128)S(1)} fusion(f32[648,2048]{1,0:T(8,128)S(1)} %shard_map.127, f32[648,16]{0,1:T(8,128)S(1)} %copy-done, f32[16]{0:T(128)S(1)} %copy-done.5), kind=kOutput, calls=%fused_computation.2 | convolution fusion | flops 127434752 | bytes 5481024 | tf_op jit(solution)/shard_map/ti,ts->is/dot_general | solution.py:744
  24.3 0.0 copy-done.4
  24.3 0.0 copy-done.6
  24.3 0.3 fusion.7
  24.6 0.0 copy-done.3
  24.6 0.8 fusion.14
  25.4 0.8 fusion.13
  26.2 0.2 concatenate.6
  26.4 0.1 copy.112
  26.5 0.0 copy-done.2
  26.5 43.6 %shard_map.128 = (f32[2,4,2,2,2,4,256]{6,5,4,3,2,1,0:T(4,128)S(1)}, f32[2,4,256]{2,1,0:T(4,128)S(1)}) custom-call(f32[2,4,2,2,2,4,256]{6,5,4,3,2,1,0:T(4,128)S(1)} %bitcast.115, f32[4,4,2,4,256]{4,3,2,1,0:T(4,128)S(1)} %bitcast.113), custom_call_target="tpu_custom_call" | custom-call | tf_op jit(solution)/shard_map/pallas_call | solution.py:545
  70.2 0.2 fusion.25
  70.4 0.4 fusion.29
  70.9 4.7 %fusion.30 = f32[16,648]{1,0:T(8,128)S(1)} fusion(f32[2048,16]{0,1:T(8,128)S(1)} %get-tuple-element.88, f32[648,2048]{1,0:T(8,128)} %copy-done.1), kind=kOutput, calls=%fused_computation.83 | convolution fusion | flops 127401984 | bytes 5480960 | tf_op jit(solution)/shard_map/is,ts->it/dot_general | solution.py:760
  75.6 0.2 fusion.31
  75.8 0.1 copy.115
  75.9 0.1 copy.113
  76.0 0.1 select_maximum_fusion
  76.1 0.1 pad.9
  76.1 11.6 %shard_map.129 = f32[128,128]{1,0:T(8,128)S(1)} custom-call(f32[128,128]{1,0:T(8,128)S(1)} %bitcast.116), custom_call_target="tpu_custom_call" | custom-call | tf_op jit(solution)/shard_map/pallas_call | solution.py:635
  87.8 0.6 slice_bitcast_fusion
  88.4 0.1 slice.146
  88.5 0.7 copy.117
  89.1 0.7 slice_reduce_fusion
  89.8 0.7 slice_reduce_fusion.1
  90.5 0.7 copy.222
  91.2 0.6 copy.223
  (15 shorter events, 0.1 us)
Async XLA Ops:
  0.6 22.3 %copy-start = (f32[648,16]{0,1:T(8,128)S(1)}, f32[648,16]{0,1:T(8,128)}, u32[]{:S(2)}) copy-start(f32[648,16]{0,1:T(8,128)} %param.12) | copy-start | bytes 124420
  0.6 22.2 %copy-start.5 = (f32[16]{0:T(128)S(1)}, f32[16]{0:T(128)}, u32[]{:S(2)}) copy-start(f32[16]{0:T(128)} %param.13) | copy-start | bytes 196
  4.0 20.3 %copy-start.4 = (f32[16,8]{0,1:T(8,128)S(1)}, f32[16,8]{0,1:T(8,128)}, u32[]{:S(2)}) copy-start(f32[16,8]{0,1:T(8,128)} %param.14) | copy-start | bytes 1540
  4.0 20.3 %copy-start.6 = (f32[8]{0:T(128)S(1)}, f32[8]{0:T(128)}, u32[]{:S(2)}) copy-start(f32[8]{0:T(128)} %param.15) | copy-start | bytes 100
  4.0 20.5 %copy-start.3 = (s32[2,4,256]{2,1,0:T(4,128)S(1)}, s32[2,4,256]{2,1,0:T(4,128)}, u32[]{:S(2)}) copy-start(s32[2,4,256]{2,1,0:T(4,128)} %param.11) | copy-start | bytes 24580
  4.0 22.5 %copy-start.2 = (f32[32,2,4,256]{3,2,1,0:T(4,128)S(1)}, f32[32,2,4,256]{3,2,1,0:T(4,128)}, u32[]{:S(2)}) copy-start(f32[32,2,4,256]{3,2,1,0:T(4,128)} %param.8) | copy-start | bytes 786436
  20.6 2.3 %copy-start.1 = (f32[648,2048]{1,0:T(8,128)}, f32[648,2048]{1,0:T(8,128)S(1)}, u32[]{:S(2)}) copy-start(f32[648,2048]{1,0:T(8,128)S(1)} %shard_map.127) | copy-start | bytes 15925252
